TPU v7x, 32 devices: a whole 2x2x4 slice. The times are simulated.
32 devices in a mesh: dp: 4 (over x, core), row: 2 (over y), col: 4 (over z).
Axes of the slice: x: 2, y: 2, z: 4, core: 2. Of those that a mesh axis runs over, the one named last changes fastest.
Arguments:
- block_input: float32 [15760, 768], P(('dp', 'row'), 'col'), may hold values from -6 to 6
- ln1_gain: float32 [768], P('col'), may hold values from 0.25 to 1.75
- ln1_bias: float32 [768], P('col'), may hold values from -3 to 3
- qkv_weight: bfloat16 [768, 2304], P('row', 'col'), may hold values from -0.21875 to 0.21875
- out_weight: bfloat16 [768, 768], P('row', 'col'), may hold values from -1.75 to 1.75
- ln2_gain: float32 [768], P('col'), may hold values from 0.25 to 1.75
- ln2_bias: float32 [768], P('col'), may hold values from -3 to 3
- router_weight: bfloat16 [768, 32], P('col'), may hold values from -0.15625 to 0.15625
- expert_in: bfloat16 [32, 768, 3072], P('row', None, 'col'), may hold values from -0.21875 to 0.21875
- expert_out: bfloat16 [32, 3072, 768], P('row', 'col'), may hold values from -1.25 to 1.25
- expert_ids: int32 [15760, 2], P(('dp', 'row')), may hold values from 0 to 31, all different within a row; in each aligned block of 1970 rows (0 to 1969, 1970 to 3939, ...) at most 168 rows name the same one
- kept_flags: int32 [15760, 2], P(('dp', 'row')), may hold values 0 or 1
- cotangent: float32 [15760, 768], P(('dp', 'row'), 'col'), may hold values from -6 to 6
Outputs:
- output: float32 [15760, 768], P(('dp', 'row'), 'col')
- grad_input: float32 [15760, 768], P(('dp', 'row'), 'col')
- grad_qkv: float32 [768, 2304], P('row', 'col')
- grad_proj: float32 [768, 768], P('row', 'col')
- grad_router: float32 [768, 32], P('col')
- grad_expert_in: float32 [32, 768, 3072], P('row', None, 'col')
- grad_expert_out: float32 [32, 3072, 768], P('row', 'col')
- grad_ln1_gain: float32 [768], P('col')
- grad_ln1_bias: float32 [768], P('col')
- grad_ln2_gain: float32 [768], P('col')
- grad_ln2_bias: float32 [768], P('col')
Inputs may be any that keep to these rules, and one draw needn't show every extreme that they name: `expert_ids`: each token names two different experts. Among the routes of the 1970 rows of one device (aligned blocks), no expert is named more than 168 times, and in some block one expert is named exactly 168 times.
All inputs are finite; a program needn't handle non-finite values. No bound on the sum of `kept_flags` on one device may be relied on, other than what follows from the above.
Results may differ from a plain program's by a relative error of at most 0.015.
Values may be sent and summed in bfloat16 or wider, within the bound.
A program may use at most 320 MiB of HBM per device.

v0:
```python
from functools import partial
import math

import jax
import jax.numpy as jnp
from jax import lax
from jax.sharding import PartitionSpec as P

HEAD_DIM = 64
E = 32
SEQ = 197
CAP = 168


EPSILON = 1e-06
CONTRACT_ROWS = (((0,), (0,)), ((), ()))
CONTRACT_COLS = (((1,), (1,)), ((), ()))


def over_rows(left, right):
    return lax.dot_general(left, right, CONTRACT_ROWS, preferred_element_type=jnp.float32)


def over_cols(left, right):
    return lax.dot_general(left, right, CONTRACT_COLS, preferred_element_type=jnp.float32)


def col_stats(summed, squares):
    return lax.psum((summed, squares), "col")


def col_total(values):
    return lax.psum(values, "col")


def col_gather(values):
    return lax.all_gather(values, "col", axis=1, tiled=True)


def col_scatter(values):
    return lax.psum_scatter(values, "col", scatter_dimension=1, tiled=True)


def routed_swap(values):
    return lax.all_to_all(values, "row", split_axis=0, concat_axis=0, tiled=True)


def normalize(values, gain_vec, bias_vec, full_width):
    summed, squares = col_stats(jnp.sum(values, axis=1), jnp.sum(values * values, axis=1))
    average = summed / full_width
    inv_std = lax.rsqrt(squares / full_width - average * average + EPSILON)
    scaled = (values - average[:, None]) * inv_std[:, None]
    return (scaled, inv_std, scaled * gain_vec + bias_vec)


def normalize_back(grad_out, scaled, inv_std, gain_vec, full_width):
    scaled_grad = grad_out * gain_vec
    summed, crossed = col_stats(jnp.sum(scaled_grad, axis=1), jnp.sum(scaled_grad * scaled, axis=1))
    grad_in = inv_std[:, None] * (
        scaled_grad - summed[:, None] / full_width - scaled * (crossed[:, None] / full_width)
    )
    return (grad_in, jnp.sum(grad_out * scaled, axis=0), jnp.sum(grad_out, axis=0))


def body(
    block_input,
    ln1_gain,
    ln1_bias,
    qkv_weight,
    out_weight,
    ln2_gain,
    ln2_bias,
    router_weight,
    expert_in,
    expert_out,
    expert_ids,
    kept_flags,
    cotangent,
):
    tokens_here, col_width = block_input.shape
    full_width = col_width * lax.axis_size("col")
    row_count = lax.axis_size("row")
    local_experts = expert_in.shape[0]
    images = tokens_here // SEQ
    score_scale = 1.0 / math.sqrt(HEAD_DIM)
    scaled_one, inv_one, normed_one = normalize(block_input, ln1_gain, ln1_bias, full_width)
    h_one_full = col_gather(normed_one.astype(jnp.bfloat16))
    qkv_full, proj_full = (
        lax.all_gather(qkv_weight, "row", axis=0, tiled=True),
        lax.all_gather(out_weight, "row", axis=0, tiled=True),
    )
    qkv_vals = jnp.dot(h_one_full, qkv_full, preferred_element_type=jnp.float32).astype(
        jnp.bfloat16
    )
    heads_here = qkv_vals.shape[1] // (3 * HEAD_DIM)
    qkv_grid = qkv_vals.reshape(images, SEQ, heads_here, 3, HEAD_DIM)
    queries = qkv_grid[:, :, :, 0]
    key_vecs = qkv_grid[:, :, :, 1]
    value_vecs = qkv_grid[:, :, :, 2]
    scores = (
        jnp.einsum("bqhd,bkhd->bhqk", queries, key_vecs, preferred_element_type=jnp.float32)
        * score_scale
    )
    largest = jnp.max(scores, axis=-1, keepdims=True)
    log_total = largest + jnp.log(jnp.sum(jnp.exp(scores - largest), axis=-1, keepdims=True))
    probs_low = jnp.exp(scores - log_total).astype(jnp.bfloat16)
    attended = jnp.einsum(
        "bhqk,bkhd->bqhd", probs_low, value_vecs, preferred_element_type=jnp.float32
    )
    attended = attended.reshape(tokens_here, heads_here * HEAD_DIM).astype(jnp.bfloat16)
    mid = block_input + col_scatter(over_cols(attended, proj_full))
    scaled_two, inv_two, normed_two = normalize(mid, ln2_gain, ln2_bias, full_width)
    h_two = normed_two.astype(jnp.bfloat16)
    logits = col_total(jnp.dot(h_two, router_weight, preferred_element_type=jnp.float32))
    route_probs = jax.nn.softmax(logits, axis=-1)
    expert_range = jnp.arange(E, dtype=jnp.int32)
    choose = expert_ids[:, :, None] == expert_range
    kept_vals = kept_flags.astype(jnp.float32)
    gate_vals = jnp.sum(jnp.where(choose, route_probs[:, None, :], 0.0), axis=2) * kept_vals
    flat_ids = expert_ids.reshape(-1)
    one_hot = (flat_ids[:, None] == expert_range).astype(jnp.int32)
    slot_index = jnp.sum(jnp.cumsum(one_hot, axis=0) * one_hot, axis=1) - 1
    target = flat_ids * CAP + slot_index
    route_total = flat_ids.shape[0]
    owners = (
        jnp.full((E * CAP,), route_total, jnp.int32)
        .at[target]
        .set(jnp.arange(route_total, dtype=jnp.int32))
    )
    dispatch = jnp.take(h_two, owners // 2, axis=0, mode="fill", fill_value=0)
    arrived = routed_swap(dispatch.reshape(row_count, -1, col_width))
    rows_in = col_gather(arrived.reshape(-1, col_width)).reshape(
        row_count, local_experts, CAP, full_width
    )
    first_full, second_full = (expert_in, expert_out)
    hidden_pre = jnp.einsum(
        "secd,edf->secf", rows_in, first_full, preferred_element_type=jnp.float32
    )
    hidden_act = jax.nn.gelu(hidden_pre, approximate=False).astype(jnp.bfloat16)
    expert_part = jnp.einsum(
        "secf,efd->secd", hidden_act, second_full, preferred_element_type=jnp.float32
    )
    returned = col_scatter(expert_part.reshape(-1, full_width)).astype(jnp.bfloat16)
    results = routed_swap(returned.reshape(row_count, -1, col_width)).reshape(E * CAP, col_width)
    routed = (
        jnp.take(results, target, axis=0).reshape(tokens_here, 2, col_width).astype(jnp.float32)
    )
    output = mid + jnp.sum(routed * gate_vals[:, :, None], axis=1)
    gate_grad = col_total(jnp.sum(cotangent[:, None, :] * routed, axis=2)) * kept_vals
    prob_grad = jnp.sum(jnp.where(choose, gate_grad[:, :, None], 0.0), axis=1)
    logit_grad = (
        route_probs * (prob_grad - jnp.sum(route_probs * prob_grad, axis=1, keepdims=True))
    ).astype(jnp.bfloat16)
    grad_router = over_rows(h_two, logit_grad)
    route_grad = (
        (cotangent[:, None, :] * gate_vals[:, :, None]).reshape(-1, col_width).astype(jnp.bfloat16)
    )
    grad_buffer = jnp.take(route_grad, owners, axis=0, mode="fill", fill_value=0)
    grad_arrived = routed_swap(grad_buffer.reshape(row_count, -1, col_width))
    grad_rows = col_gather(grad_arrived.reshape(-1, col_width)).reshape(
        row_count, local_experts, CAP, full_width
    )
    act_grad = jnp.einsum(
        "secd,efd->secf", grad_rows, second_full, preferred_element_type=jnp.float32
    )
    act_pullback = jax.vjp(partial(jax.nn.gelu, approximate=False), hidden_pre)[1]
    pre_grad = act_pullback(act_grad)[0].astype(jnp.bfloat16)
    grad_expert_out = jnp.einsum(
        "secf,secd->efd", hidden_act, grad_rows, preferred_element_type=jnp.float32
    )
    grad_expert_in = jnp.einsum(
        "secd,secf->edf", rows_in, pre_grad, preferred_element_type=jnp.float32
    )
    input_part = jnp.einsum(
        "secf,edf->secd", pre_grad, first_full, preferred_element_type=jnp.float32
    )
    grad_back = col_scatter(input_part.reshape(-1, full_width)).astype(jnp.bfloat16)
    grad_return = routed_swap(grad_back.reshape(row_count, -1, col_width)).reshape(
        E * CAP, col_width
    )
    grad_two_in = (
        jnp.take(grad_return, target, axis=0).reshape(tokens_here, 2, col_width).astype(jnp.float32)
    )
    h_two_grad = jnp.sum(grad_two_in, axis=1) + over_cols(logit_grad, router_weight)
    norm_two_grad, ln2_gain_grad, ln2_bias_grad = normalize_back(
        h_two_grad, scaled_two, inv_two, ln2_gain, full_width
    )
    mid_grad = cotangent + norm_two_grad
    mid_full = col_gather(mid_grad.astype(jnp.bfloat16))
    grad_proj = over_rows(mid_full, attended)
    att_grad = jnp.dot(mid_full, proj_full, preferred_element_type=jnp.float32).astype(jnp.bfloat16)
    att_grad = att_grad.reshape(images, SEQ, heads_here, HEAD_DIM)
    scores_again = (
        jnp.einsum("bqhd,bkhd->bhqk", queries, key_vecs, preferred_element_type=jnp.float32)
        * score_scale
    )
    att_probs = jnp.exp(scores_again - log_total)
    prob_grads = jnp.einsum(
        "bqhd,bkhd->bhqk", att_grad, value_vecs, preferred_element_type=jnp.float32
    )
    score_grad = (
        att_probs * (prob_grads - jnp.sum(att_probs * prob_grads, axis=-1, keepdims=True))
    ).astype(jnp.bfloat16)
    query_grad = (
        jnp.einsum("bhqk,bkhd->bqhd", score_grad, key_vecs, preferred_element_type=jnp.float32)
        * score_scale
    )
    key_grad = (
        jnp.einsum("bhqk,bqhd->bkhd", score_grad, queries, preferred_element_type=jnp.float32)
        * score_scale
    )
    value_grad = jnp.einsum(
        "bhqk,bqhd->bkhd",
        att_probs.astype(jnp.bfloat16),
        att_grad,
        preferred_element_type=jnp.float32,
    )
    qkv_grad = (
        jnp.stack((query_grad, key_grad, value_grad), axis=3)
        .reshape(tokens_here, -1)
        .astype(jnp.bfloat16)
    )
    grad_qkv = over_rows(h_one_full, qkv_grad)
    h_one_grad = col_scatter(over_cols(qkv_grad, qkv_full))
    norm_one_grad, ln1_gain_grad, ln1_bias_grad = normalize_back(
        h_one_grad, scaled_one, inv_one, ln1_gain, full_width
    )
    grad_input = mid_grad + norm_one_grad
    rows_here = qkv_weight.shape[0]
    totals_all = lax.psum(
        (
            grad_qkv,
            grad_proj,
            grad_router,
            ln1_gain_grad,
            ln1_bias_grad,
            ln2_gain_grad,
            ln2_bias_grad,
        ),
        ("dp", "row"),
    )
    row_start = lax.axis_index("row") * rows_here
    qkv_sum = lax.dynamic_slice_in_dim(totals_all[0], row_start, rows_here, 0)
    proj_sum = lax.dynamic_slice_in_dim(totals_all[1], row_start, rows_here, 0)
    router_sum = totals_all[2]
    gain_one = totals_all[3]
    bias_one = totals_all[4]
    gain_two = totals_all[5]
    bias_two = totals_all[6]
    expert_in_sum, expert_out_sum = lax.psum((grad_expert_in, grad_expert_out), "dp")
    return (
        output,
        grad_input,
        qkv_sum,
        proj_sum,
        router_sum,
        expert_in_sum,
        expert_out_sum,
        gain_one,
        bias_one,
        gain_two,
        bias_two,
    )


def solution(mesh):
    in_specs = (
        P(("dp", "row"), "col"),
        P("col"),
        P("col"),
        P("row", "col"),
        P("row", "col"),
        P("col"),
        P("col"),
        P("col", None),
        P("row", None, "col"),
        P("row", "col", None),
        P(("dp", "row"), None),
        P(("dp", "row"), None),
        P(("dp", "row"), "col"),
    )
    out_specs = (
        P(("dp", "row"), "col"),
        P(("dp", "row"), "col"),
        P("row", "col"),
        P("row", "col"),
        P("col", None),
        P("row", None, "col"),
        P("row", "col", None),
        P("col"),
        P("col"),
        P("col"),
        P("col"),
    )
    return jax.shard_map(body, mesh=mesh, in_specs=in_specs, out_specs=out_specs, check_vma=False)
```

profile of v0, /device:TPU:0, one launch (start us, length us, event | category | flops | bytes accessed | tf_op | source)
XLA Modules:
  0.0 3159.2 jit_solution(12836435183990536501)
XLA Ops:
  8.9 20.5 all-reduce.6
  32.8 7.4 all_gather.20
  40.2 9.0 all_gather.19
  49.2 45.4 %all-gather.5.cloned.1.call-done = bf16[1970,768]{0,1:T(8,128)(2,1)} async-done(((bf16[1970,192]{0,1:T(8,128)(2,1)}), bf16[1970,768]{0,1:T(8,128)(2,1)}) %all-gather.5.cloned.1.call-update) | async-done | bytes 3025936 | tf_op jit(solution)/shard_map/all_gather | solution.py:37
  98.5 10.0 reshape.182
  127.3 9.2 reduce-window.6
  138.8 19.4 scatter_custom_fusion
  158.9 73.0 %reduce-scatter.9.cloned.1.call-done = f32[1970,192]{0,1:T(8,128)} async-done(((f32[1970,768]{0,1:T(8,128)}), f32[1970,192]{0,1:T(8,128)}) %reduce-scatter.9.cloned.1.call-update) | async-done | bytes 1512976 | tf_op jit(solution)/shard_map/reduce_scatter | solution.py:41
  233.6 18.0 all-reduce.5
  255.2 15.8 gather_fusion
  274.6 23.7 all_to_all.20
  300.3 144.5 %all-gather.7.cloned.1.call-done = bf16[5376,768]{0,1:T(8,128)(2,1)} async-done(((bf16[5376,192]{0,1:T(8,128)(2,1)}), bf16[5376,768]{0,1:T(8,128)(2,1)}) %all-gather.7.cloned.1.call-update) | async-done | bytes 8257552 | tf_op jit(solution)/shard_map/all_gather | solution.py:37
  444.8 11.8 copy.146
  456.6 45.8 %fusion.17 = (bf16[2,16,168,768]{3,2,0,1:T(8,128)(2,1)}, f32[2,16,168,768]{3,2,0,1:T(8,128)}, f32[16,2,168,768]{3,2,1,0:T(8,128)}) fusion(bf16[16,768,768]{2,1,0:T(8,128)(2,1)} %param.23, bf16[2,16,168,768]{3,2,1,0:T(8,128)(2,1)} %bitcast.214), kind=kOutput, calls=%fused_computation.30 | convolution fusion | flops 6610157568 | bytes 68419584 | tf_op jit(solution)/shard_map/secd,edf->secf/dot_general | solution.py:136
  502.4 17.9 fusion.32
  520.3 11.3 copy.148
  531.6 17.1 copy.179
  550.8 272.4 %reduce-scatter.13.cloned.1.call-done = f32[192,5376]{1,0:T(8,128)} async-done(((f32[768,5376]{1,0:T(8,128)}), f32[192,5376]{1,0:T(8,128)}) %reduce-scatter.13.cloned.1.call-update) | async-done | bytes 4128784
  837.6 11.4 mul.254
  855.0 7.1 all-reduce.12.cloned.1.call-done
  868.9 12.3 gather_fusion.2
  886.7 17.5 psum.138
  909.5 15.8 gather_fusion.1
  928.8 21.6 all_to_all.21
  952.0 144.8 %all-gather.9.cloned.1.call-done = bf16[5376,768]{0,1:T(8,128)(2,1)} async-done(((bf16[5376,192]{0,1:T(8,128)(2,1)}), bf16[5376,768]{0,1:T(8,128)(2,1)}) %all-gather.9.cloned.1.call-update) | async-done | bytes 8257552 | tf_op jit(solution)/shard_map/all_gather | solution.py:37
  1096.9 11.9 copy.157
  1108.8 24.6 fusion.14
  1133.4 18.9 fusion.35
  1152.3 11.4 copy.159
  1163.7 17.0 copy.181
  1180.8 274.5 %reduce-scatter.15.cloned.1.call-done = f32[192,5376]{1,0:T(8,128)} async-done(((f32[768,5376]{1,0:T(8,128)}), f32[192,5376]{1,0:T(8,128)}) %reduce-scatter.15.cloned.1.call-update) | async-done | bytes 4128784
  1467.6 24.5 all-to-all-done.3
  1496.2 12.3 gather_fusion.3
  1520.0 17.9 reduce_sum.209
  1545.5 13.4 multiply_reduce_fusion.3
  1563.8 18.6 all-reduce.4
  1587.4 60.9 %all-gather.11.cloned.1.call-done = bf16[1970,768]{0,1:T(8,128)(2,1)} async-done(((bf16[1970,192]{0,1:T(8,128)(2,1)}), bf16[1970,768]{0,1:T(8,128)(2,1)}) %all-gather.11.cloned.1.call-update) | async-done | bytes 3025936 | tf_op jit(solution)/shard_map/all_gather | solution.py:37
  1674.8 7.1 convert_element_type.95
  1695.3 21.3 convolution_bitcast_fusion.1
  1716.6 21.3 convolution_bitcast_fusion
  1739.4 11.9 all-reduce.14.cloned.1.call-done
  1755.1 108.5 %reduce-scatter.11.cloned.1.call-done = f32[1970,192]{0,1:T(8,128)} async-done(((f32[1970,768]{0,1:T(8,128)}), f32[1970,192]{0,1:T(8,128)}) %reduce-scatter.11.cloned.1.call-update) | async-done | bytes 1512976 | tf_op jit(solution)/shard_map/reduce_scatter | solution.py:41
  1865.8 18.0 all-reduce.3
  1883.8 27.1 all-reduce.1
  1914.0 1189.4 %all-reduce.16.cloned.1.call-done = (f32[16,768,768]{2,1,0:T(8,128)}, f32[16,768,768]{2,1,0:T(8,128)}) async-done(((f32[16,768,768]{2,1,0:T(8,128)}, f32[16,768,768]{2,1,0:T(8,128)}), (f32[16,768,768]{2,1,0:T(8,128)}, f32[16,768,768]{2,1,0:T(8,128)})) %all-reduce.16.cloned.1.call-update) | async-done | bytes 75497488 | tf_op jit(solution)/shard_map/psum | solution.py:250
  3103.4 28.1 copy.227
  3131.5 7.7 copy-done.4
  3139.3 13.1 copy.228
  (229 shorter events, 181.6 us)
Async XLA Ops:
  7.2 542.2 %copy-start = (bf16[192,32]{0,1:T(8,128)(2,1)S(1)}, bf16[192,32]{0,1:T(8,128)(2,1)}, u32[]{:S(2)}) copy-start(bf16[192,32]{0,1:T(8,128)(2,1)} %param.22) | copy-start | bytes 36868
  7.2 25.6 copy-start.34
  7.2 33.0 %copy-start.27 = (bf16[384,576]{0,1:T(8,128)(2,1)S(1)}, bf16[384,576]{0,1:T(8,128)(2,1)}, u32[]{:S(2)}) copy-start(bf16[384,576]{0,1:T(8,128)(2,1)} %param.18) | copy-start | bytes 1327108
  7.2 87.4 %all-gather.5.cloned.1.call-start = ((), (), s32[]{:S(2)}) async-start(), calls=%async_computation.8 | async-start | bytes 3932160 | tf_op jit(solution)/shard_map/all_gather | solution.py:37
  32.7 199.1 %reduce-scatter.9.cloned.1.call-start = ((), (), s32[]{:S(2)}) async-start(), calls=%async_computation.9 | async-start | bytes 7864320 | tf_op jit(solution)/shard_map/reduce_scatter | solution.py:41
  40.2 78.3 %copy-start.22 = (bf16[768,192]{0,1:T(8,128)(2,1)}, bf16[768,192]{0,1:T(8,128)(2,1)S(1)}, u32[]{:S(2)}) copy-start(bf16[768,192]{0,1:T(8,128)(2,1)S(1)} %all_gather.20) | copy-start | bytes 884740
  49.2 49.3 %copy-start.26 = (bf16[768,576]{0,1:T(8,128)(2,1)}, bf16[768,576]{0,1:T(8,128)(2,1)S(1)}, u32[]{:S(2)}) copy-start(bf16[768,576]{0,1:T(8,128)(2,1)S(1)} %all_gather.19) | copy-start | bytes 2654212
  111.2 3.4 copy-start.15
  118.5 3.7 copy-start.20
  122.3 322.5 %all-gather.7.cloned.1.call-start = ((), (), s32[]{:S(2)}) async-start(), calls=%async_computation.10 | async-start | bytes 10321920 | tf_op jit(solution)/shard_map/all_gather | solution.py:37
  124.7 107.2 %copy-start.2 = (f32[1970,192]{0,1:T(8,128)S(1)}, f32[1970,192]{0,1:T(8,128)}, u32[]{:S(2)}) copy-start(f32[1970,192]{0,1:T(8,128)} %param.15) | copy-start | bytes 4538884
  127.1 31.8 %copy-start.28 = (s32[3940]{0:T(1024)}, s32[3940]{0:T(1024)S(1)}, u32[]{:S(2)}) copy-start(s32[3940]{0:T(1024)S(1)} %eq.35) | copy-start | bytes 47284
  136.6 115.6 %copy-start.48 = (f32[192]{0:T(256)S(1)}, f32[192]{0:T(256)}, u32[]{:S(2)}) copy-start(f32[192]{0:T(256)} %param.20) | copy-start | bytes 2308
  136.6 115.6 %copy-start.50 = (f32[192]{0:T(256)S(1)}, f32[192]{0:T(256)}, u32[]{:S(2)}) copy-start(f32[192]{0:T(256)} %param.21) | copy-start | bytes 2308
  233.6 37.4 %copy-start.5 = (f32[1970,192]{0,1:T(8,128)}, f32[1970,192]{0,1:T(8,128)S(1)}, u32[]{:S(2)}) copy-start(f32[1970,192]{0,1:T(8,128)S(1)} %get-tuple-element.51) | copy-start | bytes 4538884
  299.8 523.4 %reduce-scatter.13.cloned.1.call-start = ((), (), s32[]{:S(2)}) async-start(), calls=%async_computation.15 | async-start | bytes 20643840
  548.7 313.4 %all-reduce.12.cloned.1.call-start = ((), (), s32[]{:S(2)}) async-start(), calls=%async_computation.11 | async-start | bytes 524288 | tf_op jit(solution)/shard_map/psum | solution.py:33
  827.2 8.2 copy-start.31
  827.2 8.2 copy-start.46
  830.5 34.6 %all-to-all-start.1 = ((bf16[2,2688,192]{1,2,0:T(8,128)(2,1)}), bf16[2,2688,192]{1,2,0:T(8,128)(2,1)}, u32[]{:S(2)}, u32[]{:S(2)}) async-start(bf16[2,2688,192]{1,2,0:T(8,128)(2,1)} %copy.149), calls=%async_computation.2 | async-start | bytes 4128768 | tf_op jit(solution)/shard_map/all_to_all | solution.py:45
  835.4 261.4 %all-gather.9.cloned.1.call-start = ((), (), s32[]{:S(2)}) async-start(), calls=%async_computation.12 | async-start | bytes 10321920 | tf_op jit(solution)/shard_map/all_gather | solution.py:37
  881.2 23.0 copy-start.45
  881.2 23.0 copy-start.33
  952.0 503.3 %reduce-scatter.15.cloned.1.call-start = ((), (), s32[]{:S(2)}) async-start(), calls=%async_computation.16 | async-start | bytes 20643840
  1459.3 8.0 copy-start.17
  1462.5 29.5 all-to-all-start.3
  1467.3 181.0 %all-gather.11.cloned.1.call-start = ((), (), s32[]{:S(2)}) async-start(), calls=%async_computation.13 | async-start | bytes 3932160 | tf_op jit(solution)/shard_map/all_gather | solution.py:37
  1539.7 5.8 copy-start.10
  1545.5 16.4 copy-start.6
  1545.5 16.4 copy-start.42
  1545.5 16.4 copy-start.44
  1545.5 16.4 copy-start.49
  1582.4 65.9 %copy-start.23 = (bf16[768,192]{0,1:T(8,128)(2,1)S(1)}, bf16[768,192]{0,1:T(8,128)(2,1)}, u32[]{:S(2)}) copy-start(bf16[768,192]{0,1:T(8,128)(2,1)} %copy-done.22) | copy-start | bytes 884740
  1587.4 68.7 %copy-start.25 = (f32[10,3,197]{2,1,0:T(4,128)S(1)}, f32[10,3,197]{2,1,0:T(4,128)}, u32[]{:S(2)}) copy-start(f32[10,3,197]{2,1,0:T(4,128)} %copy-done.24) | copy-start | bytes 70924
  1587.4 163.9 %all-reduce.14.cloned.1.call-start = ((), (), s32[]{:S(2)}) async-start(), calls=%async_computation.17 | async-start | bytes 4718592 | tf_op jit(solution)/shard_map/psum | solution.py:230
  1656.1 4.3 copy-start.16
  1656.1 9.6 slice-start
  1660.4 5.3 slice-start.1
  1674.8 7.1 copy-start.21
  1681.9 4.1 copy-start.51
  1689.4 174.2 %reduce-scatter.11.cloned.1.call-start = ((), (), s32[]{:S(2)}) async-start(), calls=%async_computation.14 | async-start | bytes 7864320 | tf_op jit(solution)/shard_map/reduce_scatter | solution.py:41
  1695.2 1408.2 %all-reduce.16.cloned.1.call-start = ((), (), s32[]{:S(2)}) async-start(), calls=%async_computation.18 | async-start | bytes 150994944 | tf_op jit(solution)/shard_map/psum | solution.py:250
  1737.9 125.7 %copy-start.38 = (f32[1970]{0:T(1024)S(1)}, f32[1970]{0:T(1024)}, u32[]{:S(2)}) copy-start(f32[1970]{0:T(1024)} %copy-done.37) | copy-start | bytes 23644
  1737.9 125.7 %copy-start.40 = (f32[1970]{0:T(1024)S(1)}, f32[1970]{0:T(1024)}, u32[]{:S(2)}) copy-start(f32[1970]{0:T(1024)} %copy-done.39) | copy-start | bytes 23644
  1737.9 125.7 %copy-start.47 = (f32[192]{0:T(256)S(1)}, f32[192]{0:T(256)}, u32[]{:S(2)}) copy-start(f32[192]{0:T(256)} %param.16) | copy-start | bytes 2308
  1737.9 125.7 %copy-start.3 = (f32[1970,192]{0,1:T(8,128)S(1)}, f32[1970,192]{0,1:T(8,128)}, u32[]{:S(2)}) copy-start(f32[1970,192]{0,1:T(8,128)} %param.15) | copy-start | bytes 4538884
  1863.6 47.3 %copy-start.19 = (f32[1970,192]{0,1:T(8,128)S(1)}, f32[1970,192]{0,1:T(8,128)}, u32[]{:S(2)}) copy-start(f32[1970,192]{0,1:T(8,128)} %reduce-scatter.11.cloned.1.call-done) | copy-start | bytes 4538884
  3103.4 35.8 %copy-start.4 = (f32[16,768,768]{2,1,0:T(8,128)S(1)}, f32[16,768,768]{2,1,0:T(8,128)}, u32[]{:S(2)}) copy-start(f32[16,768,768]{2,1,0:T(8,128)} %get-tuple-element.77) | copy-start | bytes 113246208
  (19 other events, 24.1 us)
Sparse Core Ops, SparseCore 0:
  32.8 61.7 all-gather.4
  122.4 109.3 reduce-scatter.8
  299.9 144.8 all-gather.6
  548.8 274.3 reduce-scatter.12
  826.0 36.0 all-reduce.11
  952.1 144.7 all-gather.8
  1180.9 274.3 reduce-scatter.14
  1587.5 60.7 all-gather.10
  1689.5 61.6 all-reduce.13
  1753.4 110.1 reduce-scatter.10
  1866.8 1236.5 all-reduce.15
where the time goes:
time: 3170 us; the launch traced here: 3160 us
  waiting for transfers between devices  2360 us (74%)
  local copies, waits for them, and re-layouts  322 us (10%)
  matrix products  192 us (6%)
  blocking collectives  181 us (6%)
  other arithmetic  80.1 us (3%)
    psum x1, waiting for transfers between devices, body(): lax.psum((grad_expert_in, grad_expert_out), 'dp')  1190 us
    unnamed x13, waiting for transfers between devices  547 us
    all_gather x4, waiting for transfers between devices, col_gather(): return lax.all_gather(values, 'col', axis=1, tiled=True)  396 us
    reduce_scatter x2, waiting for transfers between devices, col_scatter(): return lax.psum_scatter(values, 'col', scatter_dimension=1, tiled=True)  182 us
    unnamed x117, local copies, waits for them, and re-layouts  99.7 us
    psum x4, blocking collectives, col_stats(): return lax.psum((summed, squares), 'col')  75 us
  transfers between devices with their start and end apart: 13, of which 12 were waited for; matrix products, arithmetic and copies ran while one was open for 4% of the time, Pallas kernels for 0%

commit v1 on v0

--- a/solution.py
+++ b/solution.py
@@ -10,19 +10,368 @@
 E = 32
 SEQ = 197
 CAP = 168
-
+PARTS = 4
+SIDE = 128
 
 EPSILON = 1e-06
+F32 = jnp.float32
+LOW = jnp.bfloat16
 CONTRACT_ROWS = (((0,), (0,)), ((), ()))
 CONTRACT_COLS = (((1,), (1,)), ((), ()))
 
 
 def over_rows(left, right):
-    return lax.dot_general(left, right, CONTRACT_ROWS, preferred_element_type=jnp.float32)
+    return lax.dot_general(left, right, CONTRACT_ROWS, preferred_element_type=F32)
 
 
 def over_cols(left, right):
-    return lax.dot_general(left, right, CONTRACT_COLS, preferred_element_type=jnp.float32)
+    return lax.dot_general(left, right, CONTRACT_COLS, preferred_element_type=F32)
+
+
+def matmul(left, right):
+    return jnp.dot(left, right, preferred_element_type=F32)
+
+
+def col_gather(values):
+    return lax.all_gather(values, "col", axis=1, tiled=True)
+
+
+def col_scatter(values):
+    return lax.psum_scatter(values, "col", scatter_dimension=1, tiled=True)
+
+
+def row_swap(values):
+    return lax.ppermute(values, "row", ((0, 1), (1, 0)))
+
+
+def row_gather(values):
+    if lax.axis_size("row") == 2:
+        return jnp.stack((values, row_swap(values)))
+    return lax.all_gather(values, "row", axis=0)
+
+
+def row_reduce(stacked):
+    if lax.axis_size("row") == 2:
+        return stacked[0].astype(F32) + row_swap(stacked[1]).astype(F32)
+    return lax.psum_scatter(stacked, "row", scatter_dimension=0).astype(F32)
+
+
+def own_block(stacked):
+    if lax.axis_size("row") == 2:
+        return stacked[0]
+    return lax.dynamic_index_in_dim(stacked, lax.axis_index("row"), 0, keepdims=False)
+
+
+def own_cols(values, width):
+    return lax.dynamic_slice_in_dim(values, lax.axis_index("col") * width, width, values.ndim - 1)
+
+
+def statistics(values):
+    average = jnp.mean(values, axis=-1, keepdims=True)
+    centered = values - average
+    return average, lax.rsqrt(jnp.mean(centered * centered, axis=-1, keepdims=True) + EPSILON)
+
+
+def split_low(values):
+    head = values.astype(LOW)
+    return head, (values - head.astype(F32)).astype(LOW)
+
+
+def replica_sum(into, grad, start):
+    count = lax.axis_size("dp")
+    experts = grad.shape[0]
+    if count != 4:
+        total = lax.psum(grad, "dp").astype(F32)
+        return lax.dynamic_update_slice_in_dim(into, total, start, 0)
+    core = lax.axis_index("dp") % 2
+    flat = grad.reshape(experts * 2, grad.shape[1] // 2, grad.shape[2])
+    mine = lax.dynamic_slice_in_dim(flat, core * experts, experts, 0)
+    theirs = lax.dynamic_slice_in_dim(flat, (1 - core) * experts, experts, 0)
+    beside = ((0, 1), (1, 0), (2, 3), (3, 2))
+    across = ((0, 2), (2, 0), (1, 3), (3, 1))
+    pair = (mine.astype(F32) + lax.ppermute(theirs, "dp", beside).astype(F32)).astype(LOW)
+    total = (pair.astype(F32) + lax.ppermute(pair, "dp", across).astype(F32)).astype(LOW)
+    other = lax.ppermute(total, "dp", beside)
+    into = lax.dynamic_update_slice_in_dim(into, total.astype(F32), 2 * start + core * experts, 0)
+    return lax.dynamic_update_slice_in_dim(
+        into, other.astype(F32), 2 * start + (1 - core) * experts, 0
+    )
+
+
+def body(
+    block_input,
+    ln1_gain,
+    ln1_bias,
+    qkv_weight,
+    out_weight,
+    ln2_gain,
+    ln2_bias,
+    router_weight,
+    expert_in,
+    expert_out,
+    expert_ids,
+    kept_flags,
+    cotangent,
+):
+    tokens_here, col_width = block_input.shape
+    full_width = col_width * lax.axis_size("col")
+    row_count = lax.axis_size("row")
+    local_experts = expert_in.shape[0]
+    images = tokens_here // SEQ
+    score_scale = 1.0 / math.sqrt(HEAD_DIM)
+
+    x_full = col_gather(block_input.astype(LOW))
+    vectors = col_gather(jnp.stack((ln1_gain, ln1_bias, ln2_gain, ln2_bias)))
+    gain_one, bias_one, gain_two, bias_two = vectors
+    qkv_full = lax.all_gather(qkv_weight, "row", axis=0, tiled=True)
+    proj_mine = lax.all_gather(out_weight, "row", axis=0, tiled=True)
+
+    average_one, inv_one = statistics(x_full.astype(F32))
+    h_one_full = ((x_full.astype(F32) - average_one) * inv_one * gain_one + bias_one).astype(LOW)
+    scaled_one = (block_input - average_one) * inv_one
+
+    routes = row_gather(jnp.concatenate((expert_ids, kept_flags), axis=1))
+    ids_all, kept_all = routes[:, :, :2], routes[:, :, 2:].reshape(-1, 2).astype(F32)
+    expert_range = jnp.arange(E, dtype=jnp.int32)
+    flat_ids = ids_all.reshape(row_count, -1)
+    one_hot = (flat_ids[:, :, None] == expert_range).astype(jnp.int32)
+    slot_index = jnp.sum(jnp.cumsum(one_hot, axis=1) * one_hot, axis=2) - 1
+    local_id = flat_ids - lax.axis_index("row") * local_experts
+    source = jnp.arange(row_count, dtype=jnp.int32)[:, None]
+    slot_total = local_experts * row_count * CAP
+    target = (local_id * row_count + source) * CAP + slot_index
+    is_here = (local_id >= 0) & (local_id < local_experts)
+    target = jnp.where(is_here, target, slot_total).reshape(-1)
+    route_total = target.shape[0]
+    all_tokens = route_total // 2
+    owners = (
+        jnp.full((slot_total,), route_total, jnp.int32)
+        .at[target]
+        .set(jnp.arange(route_total, dtype=jnp.int32), mode="drop")
+    )
+    slot_used = owners < route_total
+    slot_token = jnp.minimum(owners // 2, all_tokens - 1)
+
+    qkv_vals = matmul(h_one_full, qkv_full).astype(LOW)
+    heads_here = qkv_vals.shape[1] // (3 * HEAD_DIM)
+    qkv_grid = qkv_vals.reshape(images, SEQ, heads_here, 3, HEAD_DIM)
+    queries = qkv_grid[:, :, :, 0]
+    key_vecs = qkv_grid[:, :, :, 1]
+    value_vecs = qkv_grid[:, :, :, 2]
+    scores = (
+        jnp.einsum("bqhd,bkhd->bhqk", queries, key_vecs, preferred_element_type=F32) * score_scale
+    )
+    largest = jnp.max(scores, axis=-1, keepdims=True)
+    log_total = largest + jnp.log(jnp.sum(jnp.exp(scores - largest), axis=-1, keepdims=True))
+    probs_low = jnp.exp(scores - log_total).astype(LOW)
+    attended = jnp.einsum("bhqk,bkhd->bqhd", probs_low, value_vecs, preferred_element_type=F32)
+    attended = attended.reshape(tokens_here, heads_here * HEAD_DIM).astype(LOW)
+
+    cotangent_low, x_own, proj_late, router_late = lax.optimization_barrier(
+        (cotangent.astype(LOW), x_full, proj_mine, router_weight)
+    )
+    cot_full = col_gather(cotangent_low)
+    proj_full = col_gather(proj_late)
+    router_full = lax.all_gather(router_late, "col", axis=0, tiled=True)
+    x_all = row_gather(x_own).reshape(all_tokens, full_width)
+    cot_all = row_gather(cot_full).reshape(all_tokens, full_width)
+    cot_rows = jnp.take(cot_all, slot_token, axis=0, mode="clip").reshape(
+        local_experts, row_count * CAP, full_width
+    )
+
+    attended_full = col_gather(attended)
+    attended_all = row_gather(attended_full).reshape(all_tokens, full_width)
+    mid_all = x_all.astype(F32) + over_cols(attended_all, proj_full)
+    proj_cols = lax.dynamic_slice_in_dim(
+        proj_full, lax.axis_index("col") * col_width, col_width, 0
+    )
+    mid = block_input + over_cols(attended_full, proj_cols)
+    average_two, inv_two = statistics(mid_all)
+    scaled_two = (mid_all - average_two) * inv_two
+    h_two = (scaled_two * gain_two + bias_two).astype(LOW)
+    route_probs = jax.nn.softmax(matmul(h_two, router_full), axis=-1)
+    ids_flat = ids_all.reshape(-1, 2)
+    choose = ids_flat[:, :, None] == expert_range
+    kept_choose = jnp.sum(jnp.where(choose, kept_all[:, :, None], 0.0), axis=1)
+    gate_head, gate_tail = split_low(route_probs * kept_choose)
+    side = jnp.concatenate(
+        (gate_head, gate_tail, jnp.zeros((all_tokens, SIDE - 2 * E), LOW)), axis=1
+    )
+    table = jnp.concatenate((h_two, side), axis=1)
+
+    slot_token = slot_token.reshape(local_experts, -1)
+    slot_used = slot_used.reshape(local_experts, -1)
+    step = max(1, local_experts // PARTS)
+    my_experts = lax.axis_index("row") * local_experts + jnp.arange(local_experts)
+    results, backs, grads = [], [], []
+    for start in range(0, local_experts, step):
+        part = slice(start, start + step)
+        weight_in, weight_out = expert_in[part], expert_out[part]
+        fetched = jnp.take(table, slot_token[part].reshape(-1), axis=0, mode="clip").reshape(
+            step, row_count * CAP, -1
+        )
+        rows_in = fetched[:, :, :full_width]
+        gate_cols = fetched[:, :, full_width:].astype(F32)
+        named = (my_experts[part, None] == expert_range)[:, None, :]
+        gate = jnp.sum(
+            jnp.where(named, gate_cols[:, :, :E] + gate_cols[:, :, E : 2 * E], 0.0),
+            axis=2,
+            keepdims=True,
+        )
+        gate = jnp.where(slot_used[part][:, :, None], gate, 0.0)
+        cot_part = cot_rows[part]
+        pre = jnp.einsum("ecd,edf->ecf", rows_in, weight_in, preferred_element_type=F32)
+        phi = 0.5 * (1.0 + lax.erf(pre * math.sqrt(0.5)))
+        act = pre * phi
+        slope = phi + pre * (jnp.exp(-0.5 * pre * pre) * (1.0 / math.sqrt(2.0 * math.pi)))
+        back = jnp.einsum("ecd,efd->ecf", cot_part, weight_out, preferred_element_type=F32)
+        gate_back = jnp.sum(act * back, axis=2, keepdims=True)
+        pre_grad = (gate * back * slope).astype(LOW)
+        act_gated = (gate * act).astype(LOW)
+        input_part = jnp.einsum("ecf,edf->ecd", pre_grad, weight_in, preferred_element_type=F32)
+        back_head, back_tail = split_low(gate_back)
+        backs.append(
+            jnp.concatenate(
+                (
+                    input_part.astype(LOW),
+                    back_head,
+                    back_tail,
+                    jnp.zeros(gate_back.shape[:2] + (SIDE - 2,), LOW),
+                ),
+                axis=2,
+            ).reshape(-1, full_width + SIDE)
+        )
+        results.append(
+            jnp.einsum("ecf,efd->ecd", act_gated, weight_out, preferred_element_type=F32)
+            .astype(LOW)
+            .reshape(-1, full_width)
+        )
+        grads.append(
+            (
+                jnp.einsum("ecd,ecf->edf", rows_in, pre_grad, preferred_element_type=F32),
+                jnp.einsum("ecf,ecd->efd", act_gated, cot_part, preferred_element_type=F32),
+            )
+        )
+    expert_in_sum = jnp.zeros(expert_in.shape, F32)
+    expert_out_sum = jnp.zeros(expert_out.shape, F32)
+    if lax.axis_size("dp") == 4:
+        expert_in_sum = expert_in_sum.reshape(2 * local_experts, full_width // 2, -1)
+        expert_out_sum = expert_out_sum.reshape(2 * local_experts, expert_out.shape[1] // 2, -1)
+    for place, (grad_in, grad_out) in enumerate(grads):
+        expert_in_sum = replica_sum(expert_in_sum, grad_in.astype(LOW), place * step)
+        expert_out_sum = replica_sum(expert_out_sum, grad_out.astype(LOW), place * step)
+    expert_in_sum = expert_in_sum.reshape(expert_in.shape)
+    expert_out_sum = expert_out_sum.reshape(expert_out.shape)
+
+    back_rows = jnp.take(
+        jnp.concatenate(backs), target, axis=0, mode="fill", fill_value=0
+    ).reshape(all_tokens, 2, full_width + SIDE)
+    back_sum = jnp.sum(back_rows[:, :, :full_width].astype(F32), axis=1)
+    gate_grad = (
+        back_rows[:, :, full_width].astype(F32) + back_rows[:, :, full_width + 1].astype(F32)
+    ) * kept_all
+    prob_grad = jnp.sum(jnp.where(choose, gate_grad[:, :, None], 0.0), axis=1)
+    logit_grad = (
+        route_probs * (prob_grad - jnp.sum(route_probs * prob_grad, axis=1, keepdims=True))
+    ).astype(LOW)
+    grad_router = over_rows(h_two, logit_grad)
+    h_two_part = (back_sum + over_cols(logit_grad, router_full)).astype(LOW)
+    h_two_sum = col_scatter(
+        row_reduce(h_two_part.reshape(row_count, tokens_here, full_width)).astype(LOW)
+    )
+    h_two_grad = col_gather(h_two_sum).astype(F32)
+
+    result_rows = jnp.take(
+        jnp.concatenate(results), target, axis=0, mode="fill", fill_value=0
+    ).reshape(row_count, tokens_here, 2, full_width)
+    result_part = jnp.sum(result_rows.astype(F32), axis=2).astype(LOW)
+    output = mid + col_scatter(row_reduce(result_part).astype(LOW)).astype(F32)
+
+    scaled_own = own_block(scaled_two.reshape(row_count, tokens_here, full_width))
+    inv_own = own_block(inv_two.reshape(row_count, tokens_here, 1))
+    grad_two = h_two_grad * gain_two
+    norm_two_grad = inv_own * (
+        grad_two
+        - jnp.mean(grad_two, axis=1, keepdims=True)
+        - scaled_own * jnp.mean(grad_two * scaled_own, axis=1, keepdims=True)
+    )
+    ln2_gain_grad = own_cols(jnp.sum(h_two_grad * scaled_own, axis=0), col_width)
+    ln2_bias_grad = own_cols(jnp.sum(h_two_grad, axis=0), col_width)
+    mid_full = (cot_full.astype(F32) + norm_two_grad).astype(LOW)
+    mid_grad = cotangent + own_cols(norm_two_grad, col_width)
+
+    grad_proj = over_rows(mid_full, attended)
+    att_grad = matmul(mid_full, proj_mine).astype(LOW)
+    att_grad = att_grad.reshape(images, SEQ, heads_here, HEAD_DIM)
+    scores_again = (
+        jnp.einsum("bqhd,bkhd->bhqk", queries, key_vecs, preferred_element_type=F32) * score_scale
+    )
+    att_probs = jnp.exp(scores_again - log_total)
+    prob_grads = jnp.einsum("bqhd,bkhd->bhqk", att_grad, value_vecs, preferred_element_type=F32)
+    score_grad = (
+        att_probs * (prob_grads - jnp.sum(att_probs * prob_grads, axis=-1, keepdims=True))
+    ).astype(LOW)
+    query_grad = (
+        jnp.einsum("bhqk,bkhd->bqhd", score_grad, key_vecs, preferred_element_type=F32)
+        * score_scale
+    )
+    key_grad = (
+        jnp.einsum("bhqk,bqhd->bkhd", score_grad, queries, preferred_element_type=F32)
+        * score_scale
+    )
+    value_grad = jnp.einsum(
+        "bhqk,bqhd->bkhd", att_probs.astype(LOW), att_grad, preferred_element_type=F32
+    )
+    qkv_grad = (
+        jnp.stack((query_grad, key_grad, value_grad), axis=3).reshape(tokens_here, -1).astype(LOW)
+    )
+    h_one_part = over_cols(qkv_grad, qkv_full)
+    h_one_grad = col_scatter(h_one_part.astype(LOW)).astype(F32)
+    grad_qkv = over_rows(h_one_full, qkv_grad)
+
+    scaled_full = (x_full.astype(F32) - average_one) * inv_one
+    grad_one_part = h_one_part * gain_one
+    sums = lax.psum(
+        jnp.stack((jnp.sum(grad_one_part, axis=1), jnp.sum(grad_one_part * scaled_full, axis=1))),
+        "col",
+    )
+    grad_one = h_one_grad * ln1_gain
+    norm_one_grad = inv_one * (
+        grad_one
+        - sums[0][:, None] / full_width
+        - scaled_one * (sums[1][:, None] / full_width)
+    )
+    grad_input = mid_grad + norm_one_grad
+    ln1_gain_grad = jnp.sum(h_one_grad * scaled_one, axis=0)
+    ln1_bias_grad = jnp.sum(h_one_grad, axis=0)
+
+    router_sum = lax.dynamic_slice_in_dim(
+        lax.psum(grad_router, ("dp", "row", "col")), lax.axis_index("col") * col_width, col_width, 0
+    )
+    weights_sum = lax.psum(
+        lax.psum_scatter(
+            jnp.concatenate((grad_qkv, grad_proj), axis=1), "row", scatter_dimension=0, tiled=True
+        ),
+        "dp",
+    )
+    qkv_sum = weights_sum[:, : qkv_weight.shape[1]]
+    proj_sum = weights_sum[:, qkv_weight.shape[1] :]
+    vector_sums = lax.psum(
+        jnp.stack((ln1_gain_grad, ln1_bias_grad, ln2_gain_grad, ln2_bias_grad)), ("dp", "row")
+    )
+    return (
+        output,
+        grad_input,
+        qkv_sum,
+        proj_sum,
+        router_sum,
+        expert_in_sum,
+        expert_out_sum,
+        vector_sums[0],
+        vector_sums[1],
+        vector_sums[2],
+        vector_sums[3],
+    )
 
 
 def col_stats(summed, squares):
@@ -31,14 +380,6 @@
 
 def col_total(values):
     return lax.psum(values, "col")
-
-
-def col_gather(values):
-    return lax.all_gather(values, "col", axis=1, tiled=True)
-
-
-def col_scatter(values):
-    return lax.psum_scatter(values, "col", scatter_dimension=1, tiled=True)
 
 
 def routed_swap(values):
@@ -62,7 +403,7 @@
     return (grad_in, jnp.sum(grad_out * scaled, axis=0), jnp.sum(grad_out, axis=0))
 
 
-def body(
+def exchange_body(
     block_input,
     ln1_gain,
     ln1_bias,
@@ -292,4 +633,5 @@
         P("col"),
         P("col"),
     )
-    return jax.shard_map(body, mesh=mesh, in_specs=in_specs, out_specs=out_specs, check_vma=False)
+    chosen = body if mesh.shape["row"] == 2 else exchange_body
+    return jax.shard_map(chosen, mesh=mesh, in_specs=in_specs, out_specs=out_specs, check_vma=False)

time: 3170 us -> 1750 us (0.55)
  waiting for transfers between devices: 2360 us -> 466 us
  other arithmetic: 80.1 us -> 436 us
  local copies, waits for them, and re-layouts: 322 us -> 541 us
  blocking collectives: 181 us -> 74.5 us
    psum x3 -> x2, waiting for transfers between devices: 1210 us -> 0.01 us  [the longest x1 0.01 us: body(): lax.psum(grad_router, ('dp', 'row', 'col'))]
    unnamed x13, waiting for transfers between devices: 547 us -> 59 us
    ppermute x0 -> x30, waiting for transfers between devices: none -> 349 us  [the longest x8 234 us: replica_sum(): lax.ppermute(pair, 'dp', across).astype(F32)]
    all_gather x4 -> x5, waiting for transfers between devices: 396 us -> 58 us  [col_gather(): return lax.all_gather(values, 'col', axis=1, tiled=True)]
    reduce_scatter x2 -> x1, waiting for transfers between devices: 182 us -> 0.01 us  [col_scatter(): return lax.psum_scatter(values, 'col', scatter_dimension=1, tiled=True)]
    gather x6 -> x10, local copies, waits for them, and re-layouts: 62.9 us -> 239 us  [the longest x3 113 us: body(): jnp.take(jnp.concatenate(backs), target, axis=0, mode='fill', fill_value=0)]
    concatenate x0 -> x5, other arithmetic: none -> 110 us  [the longest x1 71.9 us: body(): jnp.concatenate(backs)]
    psum x6 -> x2, blocking collectives: 120 us -> 30.9 us  [the longest x1 17.2 us: body(): lax.psum(jnp.stack((jnp.sum(grad_one_part, axis=1), jnp.sum(grad_one_part...]
  transfers between devices with their start and end apart: 13 -> 41, of which waited for: 12 -> 13; matrix products, arithmetic and copies ran while one was open for 4% -> 40% of each run, Pallas kernels for 0% -> 0%
where the time goes in v1:
time: 1750 us; the launch traced here: 1740 us
  local copies, waits for them, and re-layouts  541 us (31%)
  waiting for transfers between devices  466 us (27%)
  other arithmetic  436 us (25%)
  matrix products  182 us (10%)
  blocking collectives  74.5 us (4%)
  starting transfers between devices  19.6 us (1%)
    ppermute x8, waiting for transfers between devices, replica_sum(): lax.ppermute(pair, 'dp', across).astype(F32)  234 us
    ppermute x6, waiting for transfers between devices, row_swap(): return lax.ppermute(values, 'row', ((0, 1), (1, 0)))  116 us
    gather x3, local copies, waits for them, and re-layouts, body(): jnp.take(jnp.concatenate(backs), target, axis=0, mode='fill', fill_value=0)  113 us
    concatenate x1, other arithmetic, body(): jnp.concatenate(backs)  71.9 us
    unnamed x13, waiting for transfers between devices  59 us
    gather x2, local copies, waits for them, and re-layouts, body(): jnp.take(jnp.concatenate(results), target, axis=0, mode='fill', fill_valu...  58.3 us
    all_gather x5, waiting for transfers between devices, col_gather(): return lax.all_gather(values, 'col', axis=1, tiled=True)  58 us
    gather x4, local copies, waits for them, and re-layouts, body(): jnp.take(table, slot_token[part].reshape(-1), axis=0, mode='clip')  44 us
  transfers between devices with their start and end apart: 41, of which 13 were waited for; matrix products, arithmetic and copies ran while one was open for 40% of the time, Pallas kernels for 0%

profile of v1, /device:TPU:0, one launch (start us, length us, event | category | flops | bytes accessed | tf_op | source)
XLA Modules:
  0.0 1736.6 jit_solution(7510667095221714781)
XLA Ops:
  18.5 58.0 %all-gather.8.cloned.1.call-done = bf16[1970,768]{0,1:T(8,128)(2,1)} async-done(((bf16[1970,192]{0,1:T(8,128)(2,1)}), bf16[1970,768]{0,1:T(8,128)(2,1)}) %all-gather.8.cloned.1.call-update) | async-done | bytes 3025936 | tf_op jit(solution)/shard_map/all_gather | solution.py:36
  78.2 13.2 all-gather
  91.5 9.4 all_gather.29
  110.0 11.4 reshape.625
  138.7 35.5 %reduce-window.6 = s32[2,32,31,128]{3,2,1,0:T(8,128)} reduce-window(s32[2,32,31,128]{3,2,1,0:T(8,128)} %reshape.649, s32[]{:T(128)} %constant.131.clone.1), window={size=1x1x1x128 pad=0_0x0_0x0_0x127_0}, to_apply=%region_4.5 | reduce-window | flops 32251904 | bytes 2031620 | tf_op jit(solution)/shard_map/reduce-window
  201.8 36.9 %scatter_custom_fusion = s32[5376]{0:T(1024)S(1)} fusion(s32[7880]{0:T(1024)S(1)} %fusion.135, s32[7880]{0:T(1024)S(1)} %iota.35, s32[]{:T(128)} %constant.142.clone.1), kind=kCustom, calls=%fused_computation.277 | custom fusion | bytes 21508 | tf_op jit(solution)/shard_map/scatter | solution.py:150
  251.5 13.4 all-gather.1
  269.9 8.5 maximum_convert_fusion
  278.3 12.5 copy.241
  290.8 10.2 reshape.650
  301.0 19.3 %collective-permute-done.4 = bf16[1970,768]{1,0:T(8,128)(2,1)} collective-permute-done((bf16[1970,768]{1,0:T(8,128)(2,1)S(1)}, bf16[1970,768]{1,0:T(8,128)(2,1)}, u32[]{:S(2)}, u32[]{:S(2)}) %collective-permute-start.4) | collective-permute-done | bytes 3025952 | tf_op jit(solution)/shard_map/ppermute | solution.py:44
  330.3 8.6 copy.256
  345.5 34.5 %collective-permute-done.2 = bf16[1970,768]{1,0:T(8,128)(2,1)} collective-permute-done((bf16[1970,768]{1,0:T(8,128)(2,1)}, bf16[1970,768]{1,0:T(8,128)(2,1)}, u32[]{:S(2)}, u32[]{:S(2)}) %collective-permute-start.2) | collective-permute-done | bytes 3025952 | tf_op jit(solution)/shard_map/ppermute | solution.py:44
  389.9 8.6 copy.244
  404.9 23.7 %gather_fusion.5 = bf16[5376,768]{1,0:T(8,128)(2,1)} fusion(bf16[3940,768]{1,0:T(8,128)(2,1)} %reshape.637, s32[6144]{0:T(1024)S(1)} %pad_clamp_fusion.1), kind=kCustom, calls=%fused_computation.5 | custom fusion | bytes 16536576 | tf_op jit(solution)/shard_map/jit(_take)/gather | solution.py:178
  459.4 8.4 maximum_maximum_fusion.1
  467.8 11.4 gather_fusion.3
  492.7 10.9 gather_fusion.2
  511.3 10.9 gather_fusion.1
  529.9 10.9 gather_fusion
  542.3 8.5 fusion.72
  600.5 71.9 %maximum_maximum_fusion = bf16[5376,896]{1,0:T(8,128)(2,1)} fusion(bf16[1344,126]{1,0:T(8,128)(2,1)S(1)} %concatenate.45, bf16[1344,1]{1,0:T(8,128)(2,1)S(1)} %copy-done.46, bf16[1344,1]{1,0:T(8,128)(2,1)S(1)} %copy-done.47, bf16[1344,768]{1,0:T(8,128)(2,1)S(1)} %bitcast.216, bf16[1344,1]{1,0:T(8,128)(2,1)S(1)} %copy-done.48, ...), kind=kLoop, calls=%fused_computation.16 | loop fusion | flops 154140672 | bytes 18251520 | tf_op jit(solution)/shard_map/concatenate | solution.py:267
  672.4 36.1 %gather_fusion.6 = bf16[7880,896]{1,0:T(8,128)(2,1)} fusion(bf16[5376,896]{1,0:T(8,128)(2,1)} %maximum_maximum_fusion, s32[8192]{0:T(1024)S(1)} %copy-done.60), kind=kCustom, calls=%fused_computation.6 | custom fusion | bytes 28273440 | tf_op jit(solution)/shard_map/jit(_take)/gather | solution.py:266
  708.6 28.2 %gather.37 = bf16[3940,2,896]{2,1,0:T(2,128)(2,1)} reshape(bf16[7880,896]{1,0:T(8,128)(2,1)} %gather_fusion.6) | data formatting | bytes 28241920 | tf_op jit(solution)/shard_map/jit(_take)/gather | solution.py:266
  736.7 48.6 %copy.265 = bf16[3940,2,896]{0,1,2:T(2,128)(2,1)} copy(bf16[3940,2,896]{2,1,0:T(2,128)(2,1)} %gather.37) | data formatting | bytes 28241920 | tf_op jit(solution)/shard_map/jit(_take)/gather | solution.py:266
  785.3 15.5 broadcast_select_fusion
  800.8 41.0 %convert_reduce_fusion = f32[3940,768]{0,1:T(8,128)} fusion(bf16[3940,2,896]{0,1,2:T(2,128)(2,1)} %broadcast_select_fusion), kind=kLoop, calls=%fused_computation.9 | loop fusion | flops 9077760 | bytes 24207360 | tf_op jit(solution)/shard_map/reduce_sum | solution.py:269
  841.8 12.6 copy.267
  863.3 61.8 %collective-permute-done.5 = bf16[1970,768]{1,0:T(8,128)(2,1)S(1)} collective-permute-done((bf16[1970,768]{1,0:T(8,128)(2,1)S(1)}, bf16[1970,768]{1,0:T(8,128)(2,1)S(1)}, u32[]{:S(2)}, u32[]{:S(2)}) %collective-permute-start.5) | collective-permute-done | bytes 3025952 | tf_op jit(solution)/shard_map/ppermute | solution.py:44
  930.1 58.8 %reduce-scatter.13.cloned.1.call-done = bf16[192,1970]{1,0:T(8,128)(2,1)} async-done(((bf16[768,1970]{1,0:T(8,128)(2,1)}), bf16[192,1970]{1,0:T(8,128)(2,1)}) %reduce-scatter.13.cloned.1.call-update) | async-done | bytes 756496
  1005.5 27.7 %pad_maximum_fusion = bf16[5376,768]{1,0:T(8,128)(2,1)} fusion(bf16[1344,768]{1,0:T(8,128)(2,1)S(1)} %bitcast.228, bf16[1344,768]{1,0:T(8,128)(2,1)S(1)} %bitcast.229, bf16[1344,768]{1,0:T(8,128)(2,1)S(1)} %bitcast.230, bf16[1344,768]{1,0:T(8,128)(2,1)S(1)} %bitcast.231), kind=kLoop, calls=%fused_computation.23 | loop fusion | flops 33030144 | bytes 16515072 | tf_op jit(solution)/shard_map/concatenate | solution.py:285
  1033.2 33.8 %gather_fusion.4 = bf16[7880,768]{1,0:T(8,128)(2,1)} fusion(bf16[5376,768]{1,0:T(8,128)(2,1)} %pad_maximum_fusion, s32[8192]{0:T(1024)S(1)} %copy-done.60), kind=kCustom, calls=%fused_computation.4 | custom fusion | bytes 24238880 | tf_op jit(solution)/shard_map/jit(_take)/gather | solution.py:284
  1067.0 24.5 %gather.34 = bf16[2,1970,2,768]{3,2,1,0:T(2,128)(2,1)} reshape(bf16[7880,768]{1,0:T(8,128)(2,1)} %gather_fusion.4) | data formatting | bytes 24207360 | tf_op jit(solution)/shard_map/jit(_take)/gather | solution.py:284
  1137.1 7.9 multiply_reduce_fusion.1
  1160.2 8.6 convert_element_type.644
  1174.6 40.2 %fusion = bf16[2,1970,768]{2,1,0:T(8,128)(2,1)S(1)} fusion(bf16[2,1970,2,768]{3,2,1,0:T(2,128)(2,1)} %gather.34, pred[2,1970,2]{2,1,0:T(8,128)(4,1)} %copy.236), kind=kLoop, calls=%fused_computation.14 | loop fusion | flops 9077760 | bytes 18163400 | tf_op jit(solution)/shard_map/reduce_sum | solution.py:287
  1261.8 20.1 %collective-permute-done.7 = bf16[4,384,768]{2,1,0:T(8,128)(2,1)} collective-permute-done((bf16[4,384,768]{2,1,0:T(8,128)(2,1)}, bf16[4,384,768]{2,1,0:T(8,128)(2,1)}, u32[]{:S(2)}, u32[]{:S(2)}) %collective-permute-start.7) | collective-permute-done | bytes 2359328 | tf_op jit(solution)/shard_map/ppermute | solution.py:93
  1281.8 12.7 broadcast.344.clone
  1317.1 15.7 collective-permute-done.19
  1332.8 12.7 broadcast.344.clone.1
  1368.7 15.1 collective-permute-done.10
  1398.4 35.8 %collective-permute-done.22 = bf16[4,384,768]{2,1,0:T(8,128)(2,1)S(1)} collective-permute-done((bf16[4,384,768]{2,1,0:T(8,128)(2,1)S(1)}, bf16[4,384,768]{2,1,0:T(8,128)(2,1)S(1)}, u32[]{:S(2)}, u32[]{:S(2)}) %collective-permute-start.22) | collective-permute-done | bytes 2359328 | tf_op jit(solution)/shard_map/ppermute | solution.py:93
  1460.8 24.0 %collective-permute-done.13 = bf16[4,384,768]{2,1,0:T(8,128)(2,1)} collective-permute-done((bf16[4,384,768]{2,1,0:T(8,128)(2,1)}, bf16[4,384,768]{2,1,0:T(8,128)(2,1)}, u32[]{:S(2)}, u32[]{:S(2)}) %collective-permute-start.13) | collective-permute-done | bytes 2359328 | tf_op jit(solution)/shard_map/ppermute | solution.py:93
  1507.1 47.3 %collective-permute-done.25 = bf16[4,384,768]{2,1,0:T(8,128)(2,1)} collective-permute-done((bf16[4,384,768]{2,1,0:T(8,128)(2,1)}, bf16[4,384,768]{2,1,0:T(8,128)(2,1)}, u32[]{:S(2)}, u32[]{:S(2)}) %collective-permute-start.25) | collective-permute-done | bytes 2359328 | tf_op jit(solution)/shard_map/ppermute | solution.py:93
  1569.0 35.9 %collective-permute-done.16 = bf16[4,384,768]{2,1,0:T(8,128)(2,1)} collective-permute-done((bf16[4,384,768]{2,1,0:T(8,128)(2,1)}, bf16[4,384,768]{2,1,0:T(8,128)(2,1)}, u32[]{:S(2)}, u32[]{:S(2)}) %collective-permute-start.16) | collective-permute-done | bytes 2359328 | tf_op jit(solution)/shard_map/ppermute | solution.py:93
  1615.1 40.0 %collective-permute-done.28 = bf16[4,384,768]{2,1,0:T(8,128)(2,1)} collective-permute-done((bf16[4,384,768]{2,1,0:T(8,128)(2,1)S(1)}, bf16[4,384,768]{2,1,0:T(8,128)(2,1)}, u32[]{:S(2)}, u32[]{:S(2)}) %collective-permute-start.28) | collective-permute-done | bytes 2359328 | tf_op jit(solution)/shard_map/ppermute | solution.py:93
  1675.7 17.2 psum.28
  1715.4 13.7 psum.31
  (576 shorter events, 548.5 us)
Async XLA Ops:
  7.2 70.9 %copy-start.91 = (f32[192]{0:T(256)S(1)}, f32[192]{0:T(256)}, u32[]{:S(2)}) copy-start(f32[192]{0:T(256)} %param.19) | copy-start | bytes 2308
  7.2 70.9 %copy-start.92 = (f32[192]{0:T(256)S(1)}, f32[192]{0:T(256)}, u32[]{:S(2)}) copy-start(f32[192]{0:T(256)} %param.18) | copy-start | bytes 2308
  7.2 70.9 %copy-start.93 = (f32[192]{0:T(256)S(1)}, f32[192]{0:T(256)}, u32[]{:S(2)}) copy-start(f32[192]{0:T(256)} %param.15) | copy-start | bytes 2308
  7.3 84.2 %copy-start.55 = (bf16[384,576]{0,1:T(8,128)(2,1)S(1)}, bf16[384,576]{0,1:T(8,128)(2,1)}, u32[]{:S(2)}) copy-start(bf16[384,576]{0,1:T(8,128)(2,1)} %param.16) | copy-start | bytes 1327108
  7.3 69.2 %all-gather.8.cloned.1.call-start = ((), (), s32[]{:S(2)}) async-start(), calls=%async_computation.4 | async-start | bytes 3932160 | tf_op jit(solution)/shard_map/all_gather | solution.py:36
  9.9 186.6 %all-gather.14.cloned.1.call-start = ((), (), s32[]{:S(2)}) async-start(), calls=%async_computation.8 | async-start | bytes 3932160 | tf_op jit(solution)/shard_map/all_gather | solution.py:36
  76.5 162.2 %all-gather.10.cloned.1.call-start = ((), (), s32[]{:S(2)}) async-start(), calls=%async_computation.5 | async-start | bytes 3932160 | tf_op jit(solution)/shard_map/all_gather | solution.py:36
  76.6 59.0 %collective-permute-start = (s32[1970,4]{0,1:T(4,128)S(1)}, s32[1970,4]{0,1:T(4,128)S(1)}, u32[]{:S(2)}, u32[]{:S(2)}) collective-permute-start(s32[1970,4]{0,1:T(4,128)S(1)} %get-tuple-element.147), channel_id=1, source_target_pairs={{0,4},{4,0},{1,5},{5,1},{2,6},{6,2},{3,7},{7,3},{8,12},{12,8},{9,1... | collective-permute-start | bytes 94568 | tf_op jit(solution)/shard_map/ppermute | solution.py:44
  91.5 358.3 %copy-start.69 = (f32[768]{0:T(1024)}, f32[768]{0:T(1024)S(1)}, u32[]{:S(2)}) copy-start(f32[768]{0:T(1024)S(1)} %get-tuple-element.93) | copy-start | bytes 9220
  132.1 302.5 %all-gather.12.cloned.1.call-start = ((), (), s32[]{:S(2)}) async-start(), calls=%async_computation.6 | async-start | bytes 1474560 | tf_op jit(solution)/shard_map/all_gather | solution.py:36
  186.3 78.8 %collective-permute-start.1 = (bf16[1970,768]{1,0:T(8,128)(2,1)}, bf16[1970,768]{1,0:T(8,128)(2,1)}, u32[]{:S(2)}, u32[]{:S(2)}) collective-permute-start(bf16[1970,768]{1,0:T(8,128)(2,1)} %copy.239), channel_id=1, source_target_pairs={{0,4},{4,0},{1,5},{5,1},{2,6},{6,2},{3,7},{7,3},{8,12},{12,8},{9,1... | collective-permute-start | bytes 9077768 | tf_op jit(solution)/shard_map/ppermute | solution.py:44
  200.1 120.2 %collective-permute-start.4 = (bf16[1970,768]{1,0:T(8,128)(2,1)S(1)}, bf16[1970,768]{1,0:T(8,128)(2,1)}, u32[]{:S(2)}, u32[]{:S(2)}) collective-permute-start(bf16[1970,768]{1,0:T(8,128)(2,1)S(1)} %copy.254), channel_id=1, source_target_pairs={{0,4},{4,0},{1,5},{5,1},{2,6},{6,2},{3,7},{7,3},{8,12},{12,8},{9,1... | collective-permute-start | bytes 9077768 | tf_op jit(solution)/shard_map/ppermute | solution.py:44
  243.3 136.6 %collective-permute-start.2 = (bf16[1970,768]{1,0:T(8,128)(2,1)}, bf16[1970,768]{1,0:T(8,128)(2,1)}, u32[]{:S(2)}, u32[]{:S(2)}) collective-permute-start(bf16[1970,768]{1,0:T(8,128)(2,1)} %copy.242), channel_id=1, source_target_pairs={{0,4},{4,0},{1,5},{5,1},{2,6},{6,2},{3,7},{7,3},{8,12},{12,8},{9,1... | collective-permute-start | bytes 9077768 | tf_op jit(solution)/shard_map/ppermute | solution.py:44
  251.4 737.5 %reduce-scatter.13.cloned.1.call-start = ((), (), s32[]{:S(2)}) async-start(), calls=%async_computation.13 | async-start | bytes 3932160
  265.0 190.5 %copy-start.56 = (bf16[768,32]{0,1:T(8,128)(2,1)}, bf16[768,32]{0,1:T(8,128)(2,1)S(1)}, u32[]{:S(2)}) copy-start(bf16[768,32]{0,1:T(8,128)(2,1)S(1)} %reshape.724) | copy-start | bytes 147460
  600.5 72.0 %copy-start.60 = (s32[8192]{0:T(1024)S(1)}, s32[8192]{0:T(1024)}, u32[]{:S(2)}) copy-start(s32[8192]{0:T(1024)} %pad_clamp_fusion) | copy-start | bytes 98308
  862.6 62.4 %collective-permute-start.5 = (bf16[1970,768]{1,0:T(8,128)(2,1)S(1)}, bf16[1970,768]{1,0:T(8,128)(2,1)S(1)}, u32[]{:S(2)}, u32[]{:S(2)}) collective-permute-start(bf16[1970,768]{1,0:T(8,128)(2,1)S(1)} %slice.390), channel_id=1, source_target_pairs={{0,4},{4,0},{1,5},{5,1},{2,6},{6,2},{3,7},{7,3},{8,12},{12,8},{9,1... | collective-permute-start | bytes 9077768 | tf_op jit(solution)/shard_map/ppermute | solution.py:44
  930.0 177.5 %all-gather.16.cloned.1.call-start = ((), (), s32[]{:S(2)}) async-start(), calls=%async_computation.9 | async-start | bytes 3932160 | tf_op jit(solution)/shard_map/all_gather | solution.py:36
  988.9 506.1 %reduce-scatter.11.cloned.1.call-start = ((), (), s32[]{:S(2)}) async-start(), calls=%async_computation.10 | async-start | bytes 3538944 | tf_op jit(solution)/shard_map/reduce_scatter | solution.py:352
  1099.6 123.3 %collective-permute-start.6 = (bf16[4,384,768]{2,1,0:T(8,128)(2,1)}, bf16[4,384,768]{2,1,0:T(8,128)(2,1)}, u32[]{:S(2)}, u32[]{:S(2)}) collective-permute-start(bf16[4,384,768]{2,1,0:T(8,128)(2,1)} %constant_dynamic-slice_fusion.7), channel_id=1, source_target_pairs={{0,8},{8,0},{16,24},{24,16},{1,9},{9,1},{17,25},{25,17},{2,10},{10... | collective-permute-start | bytes 7077896 | tf_op jit(solution)/shard_map/ppermute | solution.py:92
  1107.6 132.9 %collective-permute-start.18 = (bf16[4,384,768]{2,1,0:T(8,128)(2,1)}, bf16[4,384,768]{2,1,0:T(8,128)(2,1)}, u32[]{:S(2)}, u32[]{:S(2)}) collective-permute-start(bf16[4,384,768]{2,1,0:T(8,128)(2,1)} %constant_dynamic-slice_fusion.3), channel_id=1, source_target_pairs={{0,8},{8,0},{16,24},{24,16},{1,9},{9,1},{17,25},{25,17},{2,10},{10... | collective-permute-start | bytes 7077896 | tf_op jit(solution)/shard_map/ppermute | solution.py:92
  1174.5 495.2 %all-reduce.6.cloned.1.call-start = ((), (), s32[]{:S(2)}) async-start(), calls=%async_computation.12 | async-start | bytes 196608 | tf_op jit(solution)/shard_map/psum | solution.py:349
  1227.2 54.6 %collective-permute-start.7 = (bf16[4,384,768]{2,1,0:T(8,128)(2,1)}, bf16[4,384,768]{2,1,0:T(8,128)(2,1)}, u32[]{:S(2)}, u32[]{:S(2)}) collective-permute-start(bf16[4,384,768]{2,1,0:T(8,128)(2,1)} %add_convert_fusion.19), channel_id=1, source_target_pairs={{0,16},{16,0},{8,24},{24,8},{1,17},{17,1},{9,25},{25,9},{2,18},{18... | collective-permute-start | bytes 7077896 | tf_op jit(solution)/shard_map/ppermute | solution.py:93
  1233.0 71.8 %collective-permute-start.3 = (bf16[1970,768]{1,0:T(8,128)(2,1)}, bf16[1970,768]{1,0:T(8,128)(2,1)}, u32[]{:S(2)}, u32[]{:S(2)}) collective-permute-start(bf16[1970,768]{1,0:T(8,128)(2,1)} %get-tuple-element.134), channel_id=1, source_target_pairs={{0,4},{4,0},{1,5},{5,1},{2,6},{6,2},{3,7},{7,3},{8,12},{12,8},{9,1... | collective-permute-start | bytes 9077768 | tf_op jit(solution)/shard_map/ppermute | solution.py:44
  1236.1 64.4 %collective-permute-start.9 = (bf16[4,384,768]{2,1,0:T(8,128)(2,1)}, bf16[4,384,768]{2,1,0:T(8,128)(2,1)}, u32[]{:S(2)}, u32[]{:S(2)}) collective-permute-start(bf16[4,384,768]{2,1,0:T(8,128)(2,1)} %constant_dynamic-slice_fusion.6), channel_id=1, source_target_pairs={{0,8},{8,0},{16,24},{24,16},{1,9},{9,1},{17,25},{25,17},{2,10},{10... | collective-permute-start | bytes 7077896 | tf_op jit(solution)/shard_map/ppermute | solution.py:92
  1244.4 88.4 %collective-permute-start.19 = (bf16[4,384,768]{2,1,0:T(8,128)(2,1)}, bf16[4,384,768]{2,1,0:T(8,128)(2,1)}, u32[]{:S(2)}, u32[]{:S(2)}) collective-permute-start(bf16[4,384,768]{2,1,0:T(8,128)(2,1)} %add_convert_fusion.11), channel_id=1, source_target_pairs={{0,16},{16,0},{8,24},{24,8},{1,17},{17,1},{9,25},{25,9},{2,18},{18... | collective-permute-start | bytes 7077896 | tf_op jit(solution)/shard_map/ppermute | solution.py:93
  1251.6 99.1 %collective-permute-start.21 = (bf16[4,384,768]{2,1,0:T(8,128)(2,1)}, bf16[4,384,768]{2,1,0:T(8,128)(2,1)}, u32[]{:S(2)}, u32[]{:S(2)}) collective-permute-start(bf16[4,384,768]{2,1,0:T(8,128)(2,1)} %constant_dynamic-slice_fusion.2), channel_id=1, source_target_pairs={{0,8},{8,0},{16,24},{24,16},{1,9},{9,1},{17,25},{25,17},{2,10},{10... | collective-permute-start | bytes 7077896 | tf_op jit(solution)/shard_map/ppermute | solution.py:92
  1258.3 412.9 %reduce-scatter.9.cloned.1.call-start = ((), (), s32[]{:S(2)}) async-start(), calls=%async_computation.7 | async-start | bytes 3932160 | tf_op jit(solution)/shard_map/reduce_scatter | solution.py:40
  1281.8 107.9 %collective-permute-start.12 = (bf16[4,384,768]{2,1,0:T(8,128)(2,1)}, bf16[4,384,768]{2,1,0:T(8,128)(2,1)}, u32[]{:S(2)}, u32[]{:S(2)}) collective-permute-start(bf16[4,384,768]{2,1,0:T(8,128)(2,1)} %constant_dynamic-slice_fusion.5), channel_id=1, source_target_pairs={{0,8},{8,0},{16,24},{24,16},{1,9},{9,1},{17,25},{25,17},{2,10},{10... | collective-permute-start | bytes 7077896 | tf_op jit(solution)/shard_map/ppermute | solution.py:92
  1300.5 62.4 %collective-permute-start.8 = (bf16[4,384,768]{2,1,0:T(8,128)(2,1)}, bf16[4,384,768]{2,1,0:T(8,128)(2,1)}, u32[]{:S(2)}, u32[]{:S(2)}) collective-permute-start(bf16[4,384,768]{2,1,0:T(8,128)(2,1)} %get-tuple-element.112), channel_id=1, source_target_pairs={{0,8},{8,0},{16,24},{24,16},{1,9},{9,1},{17,25},{25,17},{2,10},{10... | collective-permute-start | bytes 7077896 | tf_op jit(solution)/shard_map/ppermute | solution.py:94
  1304.9 78.9 %collective-permute-start.10 = (bf16[4,384,768]{2,1,0:T(8,128)(2,1)}, bf16[4,384,768]{2,1,0:T(8,128)(2,1)}, u32[]{:S(2)}, u32[]{:S(2)}) collective-permute-start(bf16[4,384,768]{2,1,0:T(8,128)(2,1)} %add_convert_fusion.17), channel_id=1, source_target_pairs={{0,16},{16,0},{8,24},{24,8},{1,17},{17,1},{9,25},{25,9},{2,18},{18... | collective-permute-start | bytes 7077896 | tf_op jit(solution)/shard_map/ppermute | solution.py:93
  1317.1 384.6 %all-reduce.4.cloned.1.call-start = ((), (), s32[]{:S(2)}) async-start(), calls=%async_computation.11 | async-start | bytes 2359296 | tf_op jit(solution)/shard_map/psum | solution.py:351
  1350.7 43.5 %collective-permute-start.20 = (bf16[4,384,768]{2,1,0:T(8,128)(2,1)S(1)}, bf16[4,384,768]{2,1,0:T(8,128)(2,1)S(1)}, u32[]{:S(2)}, u32[]{:S(2)}) collective-permute-start(bf16[4,384,768]{2,1,0:T(8,128)(2,1)S(1)} %get-tuple-element.104), channel_id=1, source_target_pairs={{0,8},{8,0},{16,24},{24,16},{1,9},{9,1},{17,25},{25,17},{2,10},{10... | collective-permute-start | bytes 7077896 | tf_op jit(solution)/shard_map/ppermute | solution.py:94
  1353.7 80.5 %collective-permute-start.22 = (bf16[4,384,768]{2,1,0:T(8,128)(2,1)S(1)}, bf16[4,384,768]{2,1,0:T(8,128)(2,1)S(1)}, u32[]{:S(2)}, u32[]{:S(2)}) collective-permute-start(bf16[4,384,768]{2,1,0:T(8,128)(2,1)S(1)} %add_convert_fusion.9), channel_id=1, source_target_pairs={{0,16},{16,0},{8,24},{24,8},{1,17},{17,1},{9,25},{25,9},{2,18},{18... | collective-permute-start | bytes 7077896 | tf_op jit(solution)/shard_map/ppermute | solution.py:93
  1363.0 87.9 %collective-permute-start.15 = (bf16[4,384,768]{2,1,0:T(8,128)(2,1)}, bf16[4,384,768]{2,1,0:T(8,128)(2,1)}, u32[]{:S(2)}, u32[]{:S(2)}) collective-permute-start(bf16[4,384,768]{2,1,0:T(8,128)(2,1)} %constant_dynamic-slice_fusion.4), channel_id=1, source_target_pairs={{0,8},{8,0},{16,24},{24,16},{1,9},{9,1},{17,25},{25,17},{2,10},{10... | collective-permute-start | bytes 7077896 | tf_op jit(solution)/shard_map/ppermute | solution.py:92
  1383.7 60.7 %collective-permute-start.24 = (bf16[4,384,768]{2,1,0:T(8,128)(2,1)}, bf16[4,384,768]{2,1,0:T(8,128)(2,1)}, u32[]{:S(2)}, u32[]{:S(2)}) collective-permute-start(bf16[4,384,768]{2,1,0:T(8,128)(2,1)} %constant_dynamic-slice_fusion.1), channel_id=1, source_target_pairs={{0,8},{8,0},{16,24},{24,16},{1,9},{9,1},{17,25},{25,17},{2,10},{10... | collective-permute-start | bytes 7077896 | tf_op jit(solution)/shard_map/ppermute | solution.py:92
  1389.7 66.3 %collective-permute-start.11 = (bf16[4,384,768]{2,1,0:T(8,128)(2,1)}, bf16[4,384,768]{2,1,0:T(8,128)(2,1)}, u32[]{:S(2)}, u32[]{:S(2)}) collective-permute-start(bf16[4,384,768]{2,1,0:T(8,128)(2,1)} %get-tuple-element.110), channel_id=1, source_target_pairs={{0,8},{8,0},{16,24},{24,16},{1,9},{9,1},{17,25},{25,17},{2,10},{10... | collective-permute-start | bytes 7077896 | tf_op jit(solution)/shard_map/ppermute | solution.py:94
  1394.2 90.6 %collective-permute-start.13 = (bf16[4,384,768]{2,1,0:T(8,128)(2,1)}, bf16[4,384,768]{2,1,0:T(8,128)(2,1)}, u32[]{:S(2)}, u32[]{:S(2)}) collective-permute-start(bf16[4,384,768]{2,1,0:T(8,128)(2,1)} %add_convert_fusion.15), channel_id=1, source_target_pairs={{0,16},{16,0},{8,24},{24,8},{1,17},{17,1},{9,25},{25,9},{2,18},{18... | collective-permute-start | bytes 7077896 | tf_op jit(solution)/shard_map/ppermute | solution.py:93
  1437.8 53.0 %collective-permute-start.23 = (bf16[4,384,768]{2,1,0:T(8,128)(2,1)}, bf16[4,384,768]{2,1,0:T(8,128)(2,1)}, u32[]{:S(2)}, u32[]{:S(2)}) collective-permute-start(bf16[4,384,768]{2,1,0:T(8,128)(2,1)} %get-tuple-element.102), channel_id=1, source_target_pairs={{0,8},{8,0},{16,24},{24,16},{1,9},{9,1},{17,25},{25,17},{2,10},{10... | collective-permute-start | bytes 7077896 | tf_op jit(solution)/shard_map/ppermute | solution.py:94
  1444.4 115.9 %collective-permute-start.27 = (bf16[4,384,768]{2,1,0:T(8,128)(2,1)}, bf16[4,384,768]{2,1,0:T(8,128)(2,1)}, u32[]{:S(2)}, u32[]{:S(2)}) collective-permute-start(bf16[4,384,768]{2,1,0:T(8,128)(2,1)} %constant_dynamic-slice_fusion), channel_id=1, source_target_pairs={{0,8},{8,0},{16,24},{24,16},{1,9},{9,1},{17,25},{25,17},{2,10},{10... | collective-permute-start | bytes 7077896 | tf_op jit(solution)/shard_map/ppermute | solution.py:92
  1450.9 103.5 %collective-permute-start.25 = (bf16[4,384,768]{2,1,0:T(8,128)(2,1)}, bf16[4,384,768]{2,1,0:T(8,128)(2,1)}, u32[]{:S(2)}, u32[]{:S(2)}) collective-permute-start(bf16[4,384,768]{2,1,0:T(8,128)(2,1)} %add_convert_fusion.7), channel_id=1, source_target_pairs={{0,16},{16,0},{8,24},{24,8},{1,17},{17,1},{9,25},{25,9},{2,18},{18... | collective-permute-start | bytes 7077896 | tf_op jit(solution)/shard_map/ppermute | solution.py:93
  1456.0 148.9 %collective-permute-start.16 = (bf16[4,384,768]{2,1,0:T(8,128)(2,1)}, bf16[4,384,768]{2,1,0:T(8,128)(2,1)}, u32[]{:S(2)}, u32[]{:S(2)}) collective-permute-start(bf16[4,384,768]{2,1,0:T(8,128)(2,1)} %add_convert_fusion.13), channel_id=1, source_target_pairs={{0,16},{16,0},{8,24},{24,8},{1,17},{17,1},{9,25},{25,9},{2,18},{18... | collective-permute-start | bytes 7077896 | tf_op jit(solution)/shard_map/ppermute | solution.py:93
  1490.8 74.0 %collective-permute-start.14 = (bf16[4,384,768]{2,1,0:T(8,128)(2,1)}, bf16[4,384,768]{2,1,0:T(8,128)(2,1)}, u32[]{:S(2)}, u32[]{:S(2)}) collective-permute-start(bf16[4,384,768]{2,1,0:T(8,128)(2,1)} %get-tuple-element.108), channel_id=1, source_target_pairs={{0,8},{8,0},{16,24},{24,16},{1,9},{9,1},{17,25},{25,17},{2,10},{10... | collective-permute-start | bytes 7077896 | tf_op jit(solution)/shard_map/ppermute | solution.py:94
  1495.1 210.4 %reduce-scatter.15.cloned.1.call-start = ((), (), s32[]{:S(2)}) async-start(), calls=%async_computation.14 | async-start | bytes 3932160
  1560.3 50.6 %collective-permute-start.26 = (bf16[4,384,768]{2,1,0:T(8,128)(2,1)}, bf16[4,384,768]{2,1,0:T(8,128)(2,1)}, u32[]{:S(2)}, u32[]{:S(2)}) collective-permute-start(bf16[4,384,768]{2,1,0:T(8,128)(2,1)} %get-tuple-element.100), channel_id=1, source_target_pairs={{0,8},{8,0},{16,24},{24,16},{1,9},{9,1},{17,25},{25,17},{2,10},{10... | collective-permute-start | bytes 7077896 | tf_op jit(solution)/shard_map/ppermute | solution.py:94
  1563.2 91.8 %collective-permute-start.28 = (bf16[4,384,768]{2,1,0:T(8,128)(2,1)S(1)}, bf16[4,384,768]{2,1,0:T(8,128)(2,1)}, u32[]{:S(2)}, u32[]{:S(2)}) collective-permute-start(bf16[4,384,768]{2,1,0:T(8,128)(2,1)S(1)} %add_convert_fusion.5), channel_id=1, source_target_pairs={{0,16},{16,0},{8,24},{24,8},{1,17},{17,1},{9,25},{25,9},{2,18},{18... | collective-permute-start | bytes 7077896 | tf_op jit(solution)/shard_map/ppermute | solution.py:93
  1610.9 82.1 %collective-permute-start.17 = (bf16[4,384,768]{2,1,0:T(8,128)(2,1)}, bf16[4,384,768]{2,1,0:T(8,128)(2,1)}, u32[]{:S(2)}, u32[]{:S(2)}) collective-permute-start(bf16[4,384,768]{2,1,0:T(8,128)(2,1)} %get-tuple-element.106), channel_id=1, source_target_pairs={{0,8},{8,0},{16,24},{24,16},{1,9},{9,1},{17,25},{25,17},{2,10},{10... | collective-permute-start | bytes 7077896 | tf_op jit(solution)/shard_map/ppermute | solution.py:94
  1660.3 36.9 %collective-permute-start.29 = (bf16[4,384,768]{2,1,0:T(8,128)(2,1)}, bf16[4,384,768]{2,1,0:T(8,128)(2,1)}, u32[]{:S(2)}, u32[]{:S(2)}) collective-permute-start(bf16[4,384,768]{2,1,0:T(8,128)(2,1)} %get-tuple-element.98), channel_id=1, source_target_pairs={{0,8},{8,0},{16,24},{24,16},{1,9},{9,1},{17,25},{25,17},{2,10},{10... | collective-permute-start | bytes 7077896 | tf_op jit(solution)/shard_map/ppermute | solution.py:94
  (121 other events, 1382.6 us)
Sparse Core Ops, SparseCore 0:
  10.2 66.1 all-gather.7
  78.1 62.1 all-gather.13
  142.4 62.2 all-gather.9
  251.5 29.3 all-gather.11
  930.2 58.7 reduce-scatter.12
  990.3 63.5 all-gather.15
  1174.6 34.8 reduce-scatter.10
  1258.5 122.7 all-reduce.5
  1383.6 61.0 reduce-scatter.8
  1495.2 55.7 all-reduce.3
  1553.4 60.2 reduce-scatter.14

commit v2 on v1

--- a/solution.py
+++ b/solution.py
@@ -45,21 +45,17 @@
 
 
 def row_gather(values):
-    if lax.axis_size("row") == 2:
-        return jnp.stack((values, row_swap(values)))
-    return lax.all_gather(values, "row", axis=0)
-
-
-def row_reduce(stacked):
-    if lax.axis_size("row") == 2:
-        return stacked[0].astype(F32) + row_swap(stacked[1]).astype(F32)
-    return lax.psum_scatter(stacked, "row", scatter_dimension=0).astype(F32)
-
-
-def own_block(stacked):
-    if lax.axis_size("row") == 2:
-        return stacked[0]
-    return lax.dynamic_index_in_dim(stacked, lax.axis_index("row"), 0, keepdims=False)
+    return jnp.concatenate((values, row_swap(values)))
+
+
+def row_reduce(values):
+    here = values.shape[0] // 2
+    return values[:here].astype(F32) + row_swap(values[here:]).astype(F32)
+
+
+def pad_rows(values, rows, fill=0):
+    extra = jnp.full((rows - values.shape[0],) + values.shape[1:], fill, values.dtype)
+    return jnp.concatenate((values, extra))
 
 
 def own_cols(values, width):
@@ -77,21 +73,33 @@
     return head, (values - head.astype(F32)).astype(LOW)
 
 
-def replica_sum(into, grad, start):
-    count = lax.axis_size("dp")
+BESIDE = ((0, 1), (1, 0), (2, 3), (3, 2))
+ACROSS = ((0, 2), (2, 0), (1, 3), (3, 1))
+
+
+def add_beside(grad):
+    if lax.axis_size("dp") != 4:
+        return grad
     experts = grad.shape[0]
-    if count != 4:
-        total = lax.psum(grad, "dp").astype(F32)
-        return lax.dynamic_update_slice_in_dim(into, total, start, 0)
     core = lax.axis_index("dp") % 2
     flat = grad.reshape(experts * 2, grad.shape[1] // 2, grad.shape[2])
     mine = lax.dynamic_slice_in_dim(flat, core * experts, experts, 0)
     theirs = lax.dynamic_slice_in_dim(flat, (1 - core) * experts, experts, 0)
-    beside = ((0, 1), (1, 0), (2, 3), (3, 2))
-    across = ((0, 2), (2, 0), (1, 3), (3, 1))
-    pair = (mine.astype(F32) + lax.ppermute(theirs, "dp", beside).astype(F32)).astype(LOW)
-    total = (pair.astype(F32) + lax.ppermute(pair, "dp", across).astype(F32)).astype(LOW)
-    other = lax.ppermute(total, "dp", beside)
+    return (mine.astype(F32) + lax.ppermute(theirs, "dp", BESIDE).astype(F32)).astype(LOW)
+
+
+def add_across(pair):
+    if lax.axis_size("dp") != 4:
+        return lax.psum(pair, "dp")
+    return (pair.astype(F32) + lax.ppermute(pair, "dp", ACROSS).astype(F32)).astype(LOW)
+
+
+def store_both(into, total, start):
+    if lax.axis_size("dp") != 4:
+        return lax.dynamic_update_slice_in_dim(into, total.astype(F32), start, 0)
+    experts = total.shape[0]
+    core = lax.axis_index("dp") % 2
+    other = lax.ppermute(total, "dp", BESIDE)
     into = lax.dynamic_update_slice_in_dim(into, total.astype(F32), 2 * start + core * experts, 0)
     return lax.dynamic_update_slice_in_dim(
         into, other.astype(F32), 2 * start + (1 - core) * experts, 0
@@ -120,18 +128,15 @@
     images = tokens_here // SEQ
     score_scale = 1.0 / math.sqrt(HEAD_DIM)
 
-    x_full = col_gather(block_input.astype(LOW))
+    padded_tokens = -(-tokens_here // 16) * 16
+    x_full = col_gather(pad_rows(block_input.astype(LOW), padded_tokens))
     vectors = col_gather(jnp.stack((ln1_gain, ln1_bias, ln2_gain, ln2_bias)))
     gain_one, bias_one, gain_two, bias_two = vectors
     qkv_full = lax.all_gather(qkv_weight, "row", axis=0, tiled=True)
     proj_mine = lax.all_gather(out_weight, "row", axis=0, tiled=True)
 
-    average_one, inv_one = statistics(x_full.astype(F32))
-    h_one_full = ((x_full.astype(F32) - average_one) * inv_one * gain_one + bias_one).astype(LOW)
-    scaled_one = (block_input - average_one) * inv_one
-
-    routes = row_gather(jnp.concatenate((expert_ids, kept_flags), axis=1))
-    ids_all, kept_all = routes[:, :, :2], routes[:, :, 2:].reshape(-1, 2).astype(F32)
+    ids_all = row_gather(pad_rows(expert_ids, padded_tokens, E))
+    kept_all = row_gather(pad_rows(kept_flags, padded_tokens)).astype(F32)
     expert_range = jnp.arange(E, dtype=jnp.int32)
     flat_ids = ids_all.reshape(row_count, -1)
     one_hot = (flat_ids[:, :, None] == expert_range).astype(jnp.int32)
@@ -151,6 +156,22 @@
     )
     slot_used = owners < route_total
     slot_token = jnp.minimum(owners // 2, all_tokens - 1)
+    if lax.axis_size("dp") == 4:
+        expert_in_sum = jnp.zeros((2 * local_experts, expert_in.shape[1] // 2, expert_in.shape[2]), F32)
+        expert_out_sum = jnp.zeros(
+            (2 * local_experts, expert_out.shape[1] // 2, expert_out.shape[2]), F32
+        )
+    else:
+        expert_in_sum = jnp.zeros(expert_in.shape, F32)
+        expert_out_sum = jnp.zeros(expert_out.shape, F32)
+    x_padded, slot_token, slot_used, target = lax.optimization_barrier(
+        (x_full, slot_token, slot_used, target)
+    )
+    x_full = x_padded[:tokens_here]
+
+    average_one, inv_one = statistics(x_full.astype(F32))
+    h_one_full = ((x_full.astype(F32) - average_one) * inv_one * gain_one + bias_one).astype(LOW)
+    scaled_one = (block_input - average_one) * inv_one
 
     qkv_vals = matmul(h_one_full, qkv_full).astype(LOW)
     heads_here = qkv_vals.shape[1] // (3 * HEAD_DIM)
@@ -168,30 +189,29 @@
     attended = attended.reshape(tokens_here, heads_here * HEAD_DIM).astype(LOW)
 
     cotangent_low, x_own, proj_late, router_late = lax.optimization_barrier(
-        (cotangent.astype(LOW), x_full, proj_mine, router_weight)
+        (pad_rows(cotangent.astype(LOW), padded_tokens), x_padded, proj_mine, router_weight)
     )
     cot_full = col_gather(cotangent_low)
     proj_full = col_gather(proj_late)
     router_full = lax.all_gather(router_late, "col", axis=0, tiled=True)
-    x_all = row_gather(x_own).reshape(all_tokens, full_width)
-    cot_all = row_gather(cot_full).reshape(all_tokens, full_width)
+    x_all = row_gather(x_own)
+    cot_all = row_gather(cot_full)
     cot_rows = jnp.take(cot_all, slot_token, axis=0, mode="clip").reshape(
         local_experts, row_count * CAP, full_width
     )
 
-    attended_full = col_gather(attended)
-    attended_all = row_gather(attended_full).reshape(all_tokens, full_width)
+    attended_full = col_gather(pad_rows(attended, padded_tokens))
+    attended_all = row_gather(attended_full)
     mid_all = x_all.astype(F32) + over_cols(attended_all, proj_full)
     proj_cols = lax.dynamic_slice_in_dim(
         proj_full, lax.axis_index("col") * col_width, col_width, 0
     )
-    mid = block_input + over_cols(attended_full, proj_cols)
+    mid = block_input + over_cols(attended_full, proj_cols)[:tokens_here]
     average_two, inv_two = statistics(mid_all)
     scaled_two = (mid_all - average_two) * inv_two
     h_two = (scaled_two * gain_two + bias_two).astype(LOW)
     route_probs = jax.nn.softmax(matmul(h_two, router_full), axis=-1)
-    ids_flat = ids_all.reshape(-1, 2)
-    choose = ids_flat[:, :, None] == expert_range
+    choose = ids_all[:, :, None] == expert_range
     kept_choose = jnp.sum(jnp.where(choose, kept_all[:, :, None], 0.0), axis=1)
     gate_head, gate_tail = split_low(route_probs * kept_choose)
     side = jnp.concatenate(
@@ -203,7 +223,7 @@
     slot_used = slot_used.reshape(local_experts, -1)
     step = max(1, local_experts // PARTS)
     my_experts = lax.axis_index("row") * local_experts + jnp.arange(local_experts)
-    results, backs, grads = [], [], []
+    results, backs, gate_backs, grads = [], [], [], []
     for start in range(0, local_experts, step):
         part = slice(start, start + step)
         weight_in, weight_out = expert_in[part], expert_out[part]
@@ -229,18 +249,8 @@
         pre_grad = (gate * back * slope).astype(LOW)
         act_gated = (gate * act).astype(LOW)
         input_part = jnp.einsum("ecf,edf->ecd", pre_grad, weight_in, preferred_element_type=F32)
-        back_head, back_tail = split_low(gate_back)
-        backs.append(
-            jnp.concatenate(
-                (
-                    input_part.astype(LOW),
-                    back_head,
-                    back_tail,
-                    jnp.zeros(gate_back.shape[:2] + (SIDE - 2,), LOW),
-                ),
-                axis=2,
-            ).reshape(-1, full_width + SIDE)
-        )
+        backs.append(input_part.astype(LOW).reshape(-1, full_width))
+        gate_backs.append(jnp.broadcast_to(gate_back.reshape(-1, 1), (gate_back.size, SIDE)))
         results.append(
             jnp.einsum("ecf,efd->ecd", act_gated, weight_out, preferred_element_type=F32)
             .astype(LOW)
@@ -248,47 +258,45 @@
         )
         grads.append(
             (
-                jnp.einsum("ecd,ecf->edf", rows_in, pre_grad, preferred_element_type=F32),
-                jnp.einsum("ecf,ecd->efd", act_gated, cot_part, preferred_element_type=F32),
+                jnp.einsum("ecd,ecf->edf", rows_in, pre_grad, preferred_element_type=F32).astype(LOW),
+                jnp.einsum("ecf,ecd->efd", act_gated, cot_part, preferred_element_type=F32).astype(LOW),
             )
         )
-    expert_in_sum = jnp.zeros(expert_in.shape, F32)
-    expert_out_sum = jnp.zeros(expert_out.shape, F32)
-    if lax.axis_size("dp") == 4:
-        expert_in_sum = expert_in_sum.reshape(2 * local_experts, full_width // 2, -1)
-        expert_out_sum = expert_out_sum.reshape(2 * local_experts, expert_out.shape[1] // 2, -1)
-    for place, (grad_in, grad_out) in enumerate(grads):
-        expert_in_sum = replica_sum(expert_in_sum, grad_in.astype(LOW), place * step)
-        expert_out_sum = replica_sum(expert_out_sum, grad_out.astype(LOW), place * step)
-    expert_in_sum = expert_in_sum.reshape(expert_in.shape)
-    expert_out_sum = expert_out_sum.reshape(expert_out.shape)
-
-    back_rows = jnp.take(
-        jnp.concatenate(backs), target, axis=0, mode="fill", fill_value=0
-    ).reshape(all_tokens, 2, full_width + SIDE)
-    back_sum = jnp.sum(back_rows[:, :, :full_width].astype(F32), axis=1)
-    gate_grad = (
-        back_rows[:, :, full_width].astype(F32) + back_rows[:, :, full_width + 1].astype(F32)
-    ) * kept_all
+    backs, gate_backs, grads = lax.optimization_barrier((backs, gate_backs, grads))
+    pairs = [add_beside(grad) for both in grads for grad in both]
+
+    first, second = target.reshape(-1, 2).T
+
+    def fetch_both(parts):
+        rows = jnp.concatenate(parts + [jnp.zeros((16, parts[0].shape[1]), parts[0].dtype)])
+        return [jnp.take(rows, places, axis=0, mode="clip") for places in (first, second)]
+
+    back_first, back_second = fetch_both(backs)
+    gate_first, gate_second = fetch_both(gate_backs)
+    gate_grad = jnp.concatenate((gate_first[:, :1], gate_second[:, :1]), axis=1) * kept_all
     prob_grad = jnp.sum(jnp.where(choose, gate_grad[:, :, None], 0.0), axis=1)
     logit_grad = (
         route_probs * (prob_grad - jnp.sum(route_probs * prob_grad, axis=1, keepdims=True))
     ).astype(LOW)
     grad_router = over_rows(h_two, logit_grad)
-    h_two_part = (back_sum + over_cols(logit_grad, router_full)).astype(LOW)
-    h_two_sum = col_scatter(
-        row_reduce(h_two_part.reshape(row_count, tokens_here, full_width)).astype(LOW)
-    )
-    h_two_grad = col_gather(h_two_sum).astype(F32)
-
-    result_rows = jnp.take(
-        jnp.concatenate(results), target, axis=0, mode="fill", fill_value=0
-    ).reshape(row_count, tokens_here, 2, full_width)
-    result_part = jnp.sum(result_rows.astype(F32), axis=2).astype(LOW)
-    output = mid + col_scatter(row_reduce(result_part).astype(LOW)).astype(F32)
-
-    scaled_own = own_block(scaled_two.reshape(row_count, tokens_here, full_width))
-    inv_own = own_block(inv_two.reshape(row_count, tokens_here, 1))
+    h_two_part = (
+        back_first.astype(F32) + back_second.astype(F32) + over_cols(logit_grad, router_full)
+    ).astype(LOW)
+    h_two_part, pairs = lax.optimization_barrier((h_two_part, pairs))
+    h_two_sum = col_scatter(row_reduce(h_two_part).astype(LOW))
+    h_two_grad = col_gather(h_two_sum)
+    early = len(pairs) // 2
+    totals = [add_across(pair) for pair in pairs[:early]]
+    h_two_grad, totals = lax.optimization_barrier((h_two_grad, totals))
+    h_two_grad = h_two_grad[:tokens_here].astype(F32)
+
+    result_first, result_second = fetch_both(results)
+    result_part = (result_first.astype(F32) + result_second.astype(F32)).astype(LOW)
+    routed = col_scatter(row_reduce(result_part).astype(LOW))[:tokens_here]
+    output = mid + routed.astype(F32)
+
+    scaled_own = scaled_two[:tokens_here]
+    inv_own = inv_two[:tokens_here]
     grad_two = h_two_grad * gain_two
     norm_two_grad = inv_own * (
         grad_two
@@ -297,7 +305,7 @@
     )
     ln2_gain_grad = own_cols(jnp.sum(h_two_grad * scaled_own, axis=0), col_width)
     ln2_bias_grad = own_cols(jnp.sum(h_two_grad, axis=0), col_width)
-    mid_full = (cot_full.astype(F32) + norm_two_grad).astype(LOW)
+    mid_full = (cot_full[:tokens_here].astype(F32) + norm_two_grad).astype(LOW)
     mid_grad = cotangent + own_cols(norm_two_grad, col_width)
 
     grad_proj = over_rows(mid_full, attended)
@@ -325,12 +333,21 @@
     qkv_grad = (
         jnp.stack((query_grad, key_grad, value_grad), axis=3).reshape(tokens_here, -1).astype(LOW)
     )
-    h_one_part = over_cols(qkv_grad, qkv_full)
-    h_one_grad = col_scatter(h_one_part.astype(LOW)).astype(F32)
+    late = [add_across(pair) for pair in pairs[early:]]
+    h_one_part = over_cols(qkv_grad, qkv_full).astype(LOW)
+    h_one_part, totals = lax.optimization_barrier((h_one_part, totals))
+    h_one_grad = col_scatter(h_one_part).astype(F32)
+    for place, total in enumerate(totals + late):
+        if place % 2 == 0:
+            expert_in_sum = store_both(expert_in_sum, total, place // 2 * step)
+        else:
+            expert_out_sum = store_both(expert_out_sum, total, place // 2 * step)
+    expert_in_sum = expert_in_sum.reshape(expert_in.shape)
+    expert_out_sum = expert_out_sum.reshape(expert_out.shape)
     grad_qkv = over_rows(h_one_full, qkv_grad)
 
     scaled_full = (x_full.astype(F32) - average_one) * inv_one
-    grad_one_part = h_one_part * gain_one
+    grad_one_part = h_one_part.astype(F32) * gain_one
     sums = lax.psum(
         jnp.stack((jnp.sum(grad_one_part, axis=1), jnp.sum(grad_one_part * scaled_full, axis=1))),
         "col",

time: 1750 us -> 1620 us (0.926)
  other arithmetic: 436 us -> 205 us
  waiting for transfers between devices: 466 us -> 666 us
  local copies, waits for them, and re-layouts: 541 us -> 429 us
    ppermute x6 -> x7, waiting for transfers between devices: 116 us -> 254 us  [row_swap(): return lax.ppermute(values, 'row', ((0, 1), (1, 0)))]
    concatenate x3 -> x1, other arithmetic: 99.7 us -> 4.77 us  [row_gather(): return jnp.concatenate((values, row_swap(values)))]
    reduce_sum x2 -> x1, other arithmetic: 81.3 us -> 2.41 us  [body(): jnp.sum(grad_one_part, axis=1)]
    ppermute x24, waiting for transfers between devices: 234 us -> 296 us  [the longest x8 296 us: add_across(): lax.ppermute(pair, 'dp', ACROSS).astype(F32)]
    gather x5 -> x8, local copies, waits for them, and re-layouts: 171 us -> 115 us  [fetch_both(): jnp.take(rows, places, axis=0, mode='clip')]
    another operation x6 -> x3, other arithmetic: 48.8 us -> 19.4 us
    convert_element_type x5 -> x0, local copies, waits for them, and re-layouts: 23.6 us -> none  [the longest x2 22.7 us: body(): mid_all = x_all.astype(F32) + over_cols(attended_all, proj_full)]
    another operation x6 -> x5, local copies, waits for them, and re-layouts: 46.1 us -> 27.2 us
  transfers between devices with their start and end apart: 41 -> 42, of which waited for: 13 -> 13; matrix products, arithmetic and copies ran while one was open for 40% -> 35% of each run, Pallas kernels for 0% -> 0%
where the time goes in v2:
time: 1620 us; the launch traced here: 1610 us
  waiting for transfers between devices  666 us (41%)
  local copies, waits for them, and re-layouts  429 us (26%)
  other arithmetic  205 us (13%)
  matrix products  197 us (12%)
  blocking collectives  76.9 us (5%)
  starting transfers between devices  22.8 us (1%)
  between operations  16.2 us (1%)
    ppermute x8, waiting for transfers between devices, add_across(): lax.ppermute(pair, 'dp', ACROSS).astype(F32)  296 us
    ppermute x7, waiting for transfers between devices, row_swap(): return lax.ppermute(values, 'row', ((0, 1), (1, 0)))  254 us
    gather x8, local copies, waits for them, and re-layouts, fetch_both(): jnp.take(rows, places, axis=0, mode='clip')  115 us
    unnamed x13, waiting for transfers between devices  58.9 us
    all_gather x5, waiting for transfers between devices, col_gather(): return lax.all_gather(values, 'col', axis=1, tiled=True)  56.4 us
    gather x4, local copies, waits for them, and re-layouts, body(): jnp.take(table, slot_token[part].reshape(-1), axis=0, mode='clip')  44 us
    unnamed x299, local copies, waits for them, and re-layouts  40.4 us
    dynamic_update_slice x8, other arithmetic, store_both(): lax.dynamic_update_slice_in_dim(into, total.astype(F32), 2 * start + core...  36.3 us
  transfers between devices with their start and end apart: 42, of which 13 were waited for; matrix products, arithmetic and copies ran while one was open for 35% of the time, Pallas kernels for 0%

profile of v2, /device:TPU:0, one launch (start us, length us, event | category | flops | bytes accessed | tf_op | source)
XLA Modules:
  0.0 1612.9 jit_solution(12135464305690015324)
XLA Ops:
  13.6 12.4 all_gather.29
  26.1 13.6 all-gather
  50.7 18.7 %reduce-window.6 = s32[2,32,31,128]{3,2,1,0:T(8,128)S(1)} reduce-window(s32[2,32,31,128]{3,2,1,0:T(8,128)S(1)} %fusion.125, s32[]{:T(128)} %constant.124.clone.1), window={size=1x1x1x128 pad=0_0x0_0x0_0x127_0}, to_apply=%region_0.0 | reduce-window | flops 32251904 | bytes 2031620 | tf_op jit(solution)/shard_map/reduce-window
  72.2 29.6 %scatter_custom_fusion = s32[5376]{0:T(1024)S(1)} fusion(s32[7936]{0:T(1024)S(1)} %fusion.148, s32[7936]{0:T(1024)S(1)} %iota.34, s32[]{:T(128)} %constant.119.clone.1), kind=kCustom, calls=%fused_computation.290 | custom fusion | bytes 21508 | tf_op jit(solution)/shard_map/scatter | solution.py:155
  113.0 11.4 reshape.499
  145.1 56.4 %all-gather.10.cloned.1.call-done = bf16[1984,768]{0,1:T(8,128)(2,1)} async-done(((bf16[1984,192]{0,1:T(8,128)(2,1)}), bf16[1984,768]{0,1:T(8,128)(2,1)}) %all-gather.10.cloned.1.call-update) | async-done | bytes 3047440 | tf_op jit(solution)/shard_map/all_gather | solution.py:36
  201.5 15.6 copy.172
  225.5 125.2 %collective-permute-done.3 = s32[1984,2]{0,1:T(2,128)S(1)} collective-permute-done((s32[1984,2]{0,1:T(2,128)S(1)}, s32[1984,2]{0,1:T(2,128)S(1)}, u32[]{:S(2)}, u32[]{:S(2)}) %collective-permute-start.3) | collective-permute-done | bytes 15904 | tf_op jit(solution)/shard_map/ppermute | solution.py:44
  351.8 13.4 all-gather.1
  387.7 11.5 fusion.169
  414.6 8.3 maximum_maximum_fusion
  422.9 10.9 gather_fusion
  435.7 10.9 gather_fusion.1
  446.6 10.9 gather_fusion.2
  457.5 11.3 gather_fusion.3
  474.4 6.9 fusion.52
  504.7 23.7 %gather_fusion.6 = bf16[5376,768]{1,0:T(8,128)(2,1)} fusion(bf16[3968,768]{1,0:T(8,128)(2,1)} %pad_maximum_fusion, s32[6144]{0:T(1024)S(1)} %copy-done.73), kind=kCustom, calls=%fused_computation.6 | custom fusion | bytes 16536576 | tf_op jit(solution)/shard_map/jit(_take)/gather | solution.py:199
  533.4 7.9 multiply_reduce_fusion.6
  550.9 7.3 multiply_reduce_fusion.5
  570.9 6.8 multiply_reduce_fusion.4
  585.8 7.0 multiply_reduce_fusion.3
  600.5 7.2 convolution_convert_fusion.8
  623.6 8.8 gather_fusion.10
  634.6 8.4 gather_fusion.9
  669.8 20.1 %gather_fusion.8 = bf16[3968,768]{1,0:T(8,128)(2,1)} fusion(bf16[5392,768]{1,0:T(8,128)(2,1)} %constant_dynamic-update-slice_fusion.5, s32[4096]{0:T(1024)S(1)} %copy-done.66), kind=kCustom, calls=%fused_computation.8 | custom fusion | bytes 12205568 | tf_op jit(solution)/shard_map/jit(_take)/gather | solution.py:272
  689.9 20.3 %gather_fusion.7 = bf16[3968,768]{1,0:T(8,128)(2,1)} fusion(bf16[5392,768]{1,0:T(8,128)(2,1)} %constant_dynamic-update-slice_fusion.5, s32[4096]{0:T(1024)S(1)} %copy-done.65), kind=kCustom, calls=%fused_computation.7 | custom fusion | bytes 12205568 | tf_op jit(solution)/shard_map/jit(_take)/gather | solution.py:272
  710.8 6.4 add_convert_fusion
  746.3 67.3 %collective-permute-done.14 = bf16[1984,768]{1,0:T(8,128)(2,1)S(1)} collective-permute-done((bf16[1984,768]{1,0:T(8,128)(2,1)S(1)}, bf16[1984,768]{1,0:T(8,128)(2,1)S(1)}, u32[]{:S(2)}, u32[]{:S(2)}) %collective-permute-start.14) | collective-permute-done | bytes 3047456 | tf_op jit(solution)/shard_map/ppermute | solution.py:44
  818.7 58.8 %reduce-scatter.13.cloned.1.call-done = bf16[192,1984]{1,0:T(8,128)(2,1)} async-done(((bf16[768,1984]{1,0:T(8,128)(2,1)}), bf16[192,1984]{1,0:T(8,128)(2,1)}) %reduce-scatter.13.cloned.1.call-update) | async-done | bytes 761872
  906.4 30.5 %collective-permute-done.15 = bf16[4,384,768]{2,1,0:T(8,128)(2,1)S(1)} collective-permute-done((bf16[4,384,768]{2,1,0:T(8,128)(2,1)S(1)}, bf16[4,384,768]{2,1,0:T(8,128)(2,1)S(1)}, u32[]{:S(2)}, u32[]{:S(2)}) %collective-permute-start.15) | collective-permute-done | bytes 2359328 | tf_op jit(solution)/shard_map/ppermute | solution.py:94
  939.0 48.5 %collective-permute-done.16 = bf16[4,384,768]{2,1,0:T(8,128)(2,1)S(1)} collective-permute-done((bf16[4,384,768]{2,1,0:T(8,128)(2,1)S(1)}, bf16[4,384,768]{2,1,0:T(8,128)(2,1)S(1)}, u32[]{:S(2)}, u32[]{:S(2)}) %collective-permute-start.16) | collective-permute-done | bytes 2359328 | tf_op jit(solution)/shard_map/ppermute | solution.py:94
  989.6 48.5 %collective-permute-done.17 = bf16[4,384,768]{2,1,0:T(8,128)(2,1)S(1)} collective-permute-done((bf16[4,384,768]{2,1,0:T(8,128)(2,1)S(1)}, bf16[4,384,768]{2,1,0:T(8,128)(2,1)S(1)}, u32[]{:S(2)}, u32[]{:S(2)}) %collective-permute-start.17) | collective-permute-done | bytes 2359328 | tf_op jit(solution)/shard_map/ppermute | solution.py:94
  1040.1 47.2 %collective-permute-done.18 = bf16[4,384,768]{2,1,0:T(8,128)(2,1)S(1)} collective-permute-done((bf16[4,384,768]{2,1,0:T(8,128)(2,1)S(1)}, bf16[4,384,768]{2,1,0:T(8,128)(2,1)S(1)}, u32[]{:S(2)}, u32[]{:S(2)}) %collective-permute-start.18) | collective-permute-done | bytes 2359328 | tf_op jit(solution)/shard_map/ppermute | solution.py:94
  1118.6 7.9 multiply_reduce_fusion.1
  1141.6 8.3 convert_element_type.505
  1159.3 20.7 %gather_fusion.5 = bf16[3968,768]{1,0:T(8,128)(2,1)} fusion(bf16[5392,768]{1,0:T(8,128)(2,1)} %constant_dynamic-update-slice_fusion, s32[4096]{0:T(1024)S(1)} %copy-done.66), kind=kCustom, calls=%fused_computation.5 | custom fusion | bytes 12205568 | tf_op jit(solution)/shard_map/jit(_take)/gather | solution.py:272
  1180.0 20.1 %gather_fusion.4 = bf16[3968,768]{1,0:T(8,128)(2,1)} fusion(bf16[5392,768]{1,0:T(8,128)(2,1)} %constant_dynamic-update-slice_fusion, s32[4096]{0:T(1024)S(1)} %copy-done.65), kind=kCustom, calls=%fused_computation.4 | custom fusion | bytes 12205568 | tf_op jit(solution)/shard_map/jit(_take)/gather | solution.py:272
  1200.1 8.5 copy.178
  1208.7 8.5 copy.177
  1217.2 8.6 add_convert_fusion.1
  1241.2 61.3 %collective-permute-done.4 = bf16[1984,768]{1,0:T(8,128)(2,1)} collective-permute-done((bf16[1984,768]{1,0:T(8,128)(2,1)}, bf16[1984,768]{1,0:T(8,128)(2,1)}, u32[]{:S(2)}, u32[]{:S(2)}) %collective-permute-start.4) | collective-permute-done | bytes 3047456 | tf_op jit(solution)/shard_map/ppermute | solution.py:44
  1327.2 12.7 broadcast.333.clone
  1344.2 12.7 broadcast.333.clone.1
  1389.9 35.8 %collective-permute-done.27 = bf16[4,384,768]{2,1,0:T(8,128)(2,1)} collective-permute-done((bf16[4,384,768]{2,1,0:T(8,128)(2,1)}, bf16[4,384,768]{2,1,0:T(8,128)(2,1)}, u32[]{:S(2)}, u32[]{:S(2)}) %collective-permute-start.27) | collective-permute-done | bytes 2359328 | tf_op jit(solution)/shard_map/ppermute | solution.py:94
  1449.1 46.1 %collective-permute-done.23 = bf16[4,384,768]{2,1,0:T(8,128)(2,1)} collective-permute-done((bf16[4,384,768]{2,1,0:T(8,128)(2,1)}, bf16[4,384,768]{2,1,0:T(8,128)(2,1)}, u32[]{:S(2)}, u32[]{:S(2)}) %collective-permute-start.23) | collective-permute-done | bytes 2359328 | tf_op jit(solution)/shard_map/ppermute | solution.py:94
  1505.4 39.4 %collective-permute-done.29 = bf16[4,384,768]{2,1,0:T(8,128)(2,1)} collective-permute-done((bf16[4,384,768]{2,1,0:T(8,128)(2,1)}, bf16[4,384,768]{2,1,0:T(8,128)(2,1)}, u32[]{:S(2)}, u32[]{:S(2)}) %collective-permute-start.29) | collective-permute-done | bytes 2359328 | tf_op jit(solution)/shard_map/ppermute | solution.py:94
  1553.3 18.3 %psum.28 = f32[2,1970]{1,0:T(2,128)S(1)} all-reduce(f32[2,1970]{1,0:T(2,128)S(1)} %pad_maximum_fusion.3), channel_id=1, replica_groups=mesh['dp'=4,'row'=2,'col'=4] {'col'}, use_global_device_ids=true, to_apply=%region_31.32 | all-reduce | flops 3940 | bytes 31520 | tf_op jit(solution)/shard_map/psum | solution.py:351
  1583.8 13.2 psum.31
  (605 shorter events, 483.0 us)
Async XLA Ops:
  7.2 96.4 %all-gather.8.cloned.1.call-start = ((), (), s32[]{:S(2)}) async-start(), calls=%async_computation.4 | async-start | bytes 3932160 | tf_op jit(solution)/shard_map/all_gather | solution.py:36
  8.1 32.4 %collective-permute-start = (s32[1984,2]{0,1:T(2,128)S(1)}, s32[1984,2]{0,1:T(2,128)S(1)}, u32[]{:S(2)}, u32[]{:S(2)}) collective-permute-start(s32[1984,2]{0,1:T(2,128)S(1)} %concatenate.64), channel_id=1, source_target_pairs={{0,4},{4,0},{1,5},{5,1},{2,6},{6,2},{3,7},{7,3},{8,12},{12,8},{9,1... | collective-permute-start | bytes 47624 | tf_op jit(solution)/shard_map/ppermute | solution.py:44
  13.6 187.9 %all-gather.10.cloned.1.call-start = ((), (), s32[]{:S(2)}) async-start(), calls=%async_computation.5 | async-start | bytes 3932160 | tf_op jit(solution)/shard_map/all_gather | solution.py:36
  40.4 68.4 %copy-start.85 = (f32[768]{0:T(1024)}, f32[768]{0:T(1024)S(1)}, u32[]{:S(2)}) copy-start(f32[768]{0:T(1024)S(1)} %get-tuple-element.165) | copy-start | bytes 9220
  40.4 68.4 %copy-start.93 = (f32[768]{0:T(1024)}, f32[768]{0:T(1024)S(1)}, u32[]{:S(2)}) copy-start(f32[768]{0:T(1024)S(1)} %get-tuple-element.164) | copy-start | bytes 9220
  137.8 240.1 %all-gather.14.cloned.1.call-start = ((), (), s32[]{:S(2)}) async-start(), calls=%async_computation.8 | async-start | bytes 3932160 | tf_op jit(solution)/shard_map/all_gather | solution.py:36
  138.0 80.6 %copy-start.10 = (bf16[1984,768]{0,1:T(8,128)(2,1)S(1)}, bf16[1984,768]{0,1:T(8,128)(2,1)}, u32[]{:S(2)}) copy-start(bf16[1984,768]{0,1:T(8,128)(2,1)} %all-gather.8.cloned.1.call-done) | copy-start | bytes 9142276
  145.1 242.6 %all-gather.12.cloned.1.call-start = ((), (), s32[]{:S(2)}) async-start(), calls=%async_computation.6 | async-start | bytes 1474560 | tf_op jit(solution)/shard_map/all_gather | solution.py:36
  217.1 165.9 %collective-permute-start.2 = (bf16[1984,768]{1,0:T(8,128)(2,1)}, bf16[1984,768]{1,0:T(8,128)(2,1)}, u32[]{:S(2)}, u32[]{:S(2)}) collective-permute-start(bf16[1984,768]{1,0:T(8,128)(2,1)} %copy.172), channel_id=1, source_target_pairs={{0,4},{4,0},{1,5},{5,1},{2,6},{6,2},{3,7},{7,3},{8,12},{12,8},{9,1... | collective-permute-start | bytes 9142280 | tf_op jit(solution)/shard_map/ppermute | solution.py:44
  221.4 166.3 %collective-permute-start.1 = (bf16[1984,768]{1,0:T(8,128)(2,1)}, bf16[1984,768]{1,0:T(8,128)(2,1)}, u32[]{:S(2)}, u32[]{:S(2)}) collective-permute-start(bf16[1984,768]{1,0:T(8,128)(2,1)} %copy.171), channel_id=1, source_target_pairs={{0,4},{4,0},{1,5},{5,1},{2,6},{6,2},{3,7},{7,3},{8,12},{12,8},{9,1... | collective-permute-start | bytes 9142280 | tf_op jit(solution)/shard_map/ppermute | solution.py:44
  221.9 128.8 %collective-permute-start.3 = (s32[1984,2]{0,1:T(2,128)S(1)}, s32[1984,2]{0,1:T(2,128)S(1)}, u32[]{:S(2)}, u32[]{:S(2)}) collective-permute-start(s32[1984,2]{0,1:T(2,128)S(1)} %concatenate.71), channel_id=1, source_target_pairs={{0,4},{4,0},{1,5},{5,1},{2,6},{6,2},{3,7},{7,3},{8,12},{12,8},{9,1... | collective-permute-start | bytes 47624 | tf_op jit(solution)/shard_map/ppermute | solution.py:44
  223.5 654.0 %reduce-scatter.13.cloned.1.call-start = ((), (), s32[]{:S(2)}) async-start(), calls=%async_computation.13 | async-start | bytes 3932160
  381.5 118.4 %copy-start.3 = (bf16[1984,768]{1,0:T(8,128)(2,1)}, bf16[1984,768]{1,0:T(8,128)(2,1)S(1)}, u32[]{:S(2)}) copy-start(bf16[1984,768]{1,0:T(8,128)(2,1)S(1)} %copy.182) | copy-start | bytes 9142276
  381.5 118.4 %collective-permute-start.5 = (bf16[1984,768]{1,0:T(8,128)(2,1)S(1)}, bf16[1984,768]{1,0:T(8,128)(2,1)}, u32[]{:S(2)}, u32[]{:S(2)}) collective-permute-start(bf16[1984,768]{1,0:T(8,128)(2,1)S(1)} %copy.182), channel_id=1, source_target_pairs={{0,4},{4,0},{1,5},{5,1},{2,6},{6,2},{3,7},{7,3},{8,12},{12,8},{9,1... | collective-permute-start | bytes 9142280 | tf_op jit(solution)/shard_map/ppermute | solution.py:44
  532.3 53.5 %copy-start.46 = (bf16[1344,768]{1,0:T(8,128)(2,1)}, bf16[1344,768]{1,0:T(8,128)(2,1)S(1)}, u32[]{:S(2)}) copy-start(bf16[1344,768]{1,0:T(8,128)(2,1)S(1)} %get-tuple-element.184) | copy-start | bytes 6193156
  648.6 61.6 %collective-permute-start.6 = (bf16[4,384,768]{2,1,0:T(8,128)(2,1)}, bf16[4,384,768]{2,1,0:T(8,128)(2,1)S(1)}, u32[]{:S(2)}, u32[]{:S(2)}) collective-permute-start(bf16[4,384,768]{2,1,0:T(8,128)(2,1)} %constant_dynamic-slice_fusion.8), channel_id=1, source_target_pairs={{0,8},{8,0},{16,24},{24,16},{1,9},{9,1},{17,25},{25,17},{2,10},{10... | collective-permute-start | bytes 7077896 | tf_op jit(solution)/shard_map/ppermute | solution.py:88
  652.1 58.2 %collective-permute-start.7 = (bf16[4,384,768]{2,1,0:T(8,128)(2,1)}, bf16[4,384,768]{2,1,0:T(8,128)(2,1)}, u32[]{:S(2)}, u32[]{:S(2)}) collective-permute-start(bf16[4,384,768]{2,1,0:T(8,128)(2,1)} %constant_dynamic-slice_fusion.7), channel_id=1, source_target_pairs={{0,8},{8,0},{16,24},{24,16},{1,9},{9,1},{17,25},{25,17},{2,10},{10... | collective-permute-start | bytes 7077896 | tf_op jit(solution)/shard_map/ppermute | solution.py:88
  654.2 65.1 %collective-permute-start.8 = (bf16[4,384,768]{2,1,0:T(8,128)(2,1)}, bf16[4,384,768]{2,1,0:T(8,128)(2,1)}, u32[]{:S(2)}, u32[]{:S(2)}) collective-permute-start(bf16[4,384,768]{2,1,0:T(8,128)(2,1)} %constant_dynamic-slice_fusion.6), channel_id=1, source_target_pairs={{0,8},{8,0},{16,24},{24,16},{1,9},{9,1},{17,25},{25,17},{2,10},{10... | collective-permute-start | bytes 7077896 | tf_op jit(solution)/shard_map/ppermute | solution.py:88
  658.1 73.4 %collective-permute-start.9 = (bf16[4,384,768]{2,1,0:T(8,128)(2,1)}, bf16[4,384,768]{2,1,0:T(8,128)(2,1)}, u32[]{:S(2)}, u32[]{:S(2)}) collective-permute-start(bf16[4,384,768]{2,1,0:T(8,128)(2,1)} %constant_dynamic-slice_fusion.5), channel_id=1, source_target_pairs={{0,8},{8,0},{16,24},{24,16},{1,9},{9,1},{17,25},{25,17},{2,10},{10... | collective-permute-start | bytes 7077896 | tf_op jit(solution)/shard_map/ppermute | solution.py:88
  659.8 75.5 %collective-permute-start.10 = (bf16[4,384,768]{2,1,0:T(8,128)(2,1)}, bf16[4,384,768]{2,1,0:T(8,128)(2,1)}, u32[]{:S(2)}, u32[]{:S(2)}) collective-permute-start(bf16[4,384,768]{2,1,0:T(8,128)(2,1)} %constant_dynamic-slice_fusion.4), channel_id=1, source_target_pairs={{0,8},{8,0},{16,24},{24,16},{1,9},{9,1},{17,25},{25,17},{2,10},{10... | collective-permute-start | bytes 7077896 | tf_op jit(solution)/shard_map/ppermute | solution.py:88
  710.2 28.9 %collective-permute-start.11 = (bf16[4,384,768]{2,1,0:T(8,128)(2,1)}, bf16[4,384,768]{2,1,0:T(8,128)(2,1)S(1)}, u32[]{:S(2)}, u32[]{:S(2)}) collective-permute-start(bf16[4,384,768]{2,1,0:T(8,128)(2,1)} %constant_dynamic-slice_fusion.3), channel_id=1, source_target_pairs={{0,8},{8,0},{16,24},{24,16},{1,9},{9,1},{17,25},{25,17},{2,10},{10... | collective-permute-start | bytes 7077896 | tf_op jit(solution)/shard_map/ppermute | solution.py:88
  710.3 30.8 %collective-permute-start.12 = (bf16[4,384,768]{2,1,0:T(8,128)(2,1)}, bf16[4,384,768]{2,1,0:T(8,128)(2,1)S(1)}, u32[]{:S(2)}, u32[]{:S(2)}) collective-permute-start(bf16[4,384,768]{2,1,0:T(8,128)(2,1)} %constant_dynamic-slice_fusion.2), channel_id=1, source_target_pairs={{0,8},{8,0},{16,24},{24,16},{1,9},{9,1},{17,25},{25,17},{2,10},{10... | collective-permute-start | bytes 7077896 | tf_op jit(solution)/shard_map/ppermute | solution.py:88
  719.2 23.8 %collective-permute-start.13 = (bf16[4,384,768]{2,1,0:T(8,128)(2,1)S(1)}, bf16[4,384,768]{2,1,0:T(8,128)(2,1)S(1)}, u32[]{:S(2)}, u32[]{:S(2)}) collective-permute-start(bf16[4,384,768]{2,1,0:T(8,128)(2,1)S(1)} %constant_dynamic-slice_fusion.1), channel_id=1, source_target_pairs={{0,8},{8,0},{16,24},{24,16},{1,9},{9,1},{17,25},{25,17},{2,10},{10... | collective-permute-start | bytes 7077896 | tf_op jit(solution)/shard_map/ppermute | solution.py:88
  745.3 68.4 %collective-permute-start.14 = (bf16[1984,768]{1,0:T(8,128)(2,1)S(1)}, bf16[1984,768]{1,0:T(8,128)(2,1)S(1)}, u32[]{:S(2)}, u32[]{:S(2)}) collective-permute-start(bf16[1984,768]{1,0:T(8,128)(2,1)S(1)} %slice.309), channel_id=1, source_target_pairs={{0,4},{4,0},{1,5},{5,1},{2,6},{6,2},{3,7},{7,3},{8,12},{12,8},{9,1... | collective-permute-start | bytes 9142280 | tf_op jit(solution)/shard_map/ppermute | solution.py:44
  818.7 270.6 %all-gather.16.cloned.1.call-start = ((), (), s32[]{:S(2)}) async-start(), calls=%async_computation.9 | async-start | bytes 3932160 | tf_op jit(solution)/shard_map/all_gather | solution.py:36
  877.5 442.5 %reduce-scatter.11.cloned.1.call-start = ((), (), s32[]{:S(2)}) async-start(), calls=%async_computation.10 | async-start | bytes 3538944 | tf_op jit(solution)/shard_map/reduce_scatter | solution.py:369
  882.7 54.2 %collective-permute-start.15 = (bf16[4,384,768]{2,1,0:T(8,128)(2,1)S(1)}, bf16[4,384,768]{2,1,0:T(8,128)(2,1)S(1)}, u32[]{:S(2)}, u32[]{:S(2)}) collective-permute-start(bf16[4,384,768]{2,1,0:T(8,128)(2,1)S(1)} %copy-done.17), channel_id=1, source_target_pairs={{0,16},{16,0},{8,24},{24,8},{1,17},{17,1},{9,25},{25,9},{2,18},{18... | collective-permute-start | bytes 7077896 | tf_op jit(solution)/shard_map/ppermute | solution.py:94
  889.3 98.2 %collective-permute-start.16 = (bf16[4,384,768]{2,1,0:T(8,128)(2,1)S(1)}, bf16[4,384,768]{2,1,0:T(8,128)(2,1)S(1)}, u32[]{:S(2)}, u32[]{:S(2)}) collective-permute-start(bf16[4,384,768]{2,1,0:T(8,128)(2,1)S(1)} %copy-done.16), channel_id=1, source_target_pairs={{0,16},{16,0},{8,24},{24,8},{1,17},{17,1},{9,25},{25,9},{2,18},{18... | collective-permute-start | bytes 7077896 | tf_op jit(solution)/shard_map/ppermute | solution.py:94
  889.4 148.6 %collective-permute-start.17 = (bf16[4,384,768]{2,1,0:T(8,128)(2,1)S(1)}, bf16[4,384,768]{2,1,0:T(8,128)(2,1)S(1)}, u32[]{:S(2)}, u32[]{:S(2)}) collective-permute-start(bf16[4,384,768]{2,1,0:T(8,128)(2,1)S(1)} %copy-done.14), channel_id=1, source_target_pairs={{0,16},{16,0},{8,24},{24,8},{1,17},{17,1},{9,25},{25,9},{2,18},{18... | collective-permute-start | bytes 7077896 | tf_op jit(solution)/shard_map/ppermute | solution.py:94
  898.0 189.3 %collective-permute-start.18 = (bf16[4,384,768]{2,1,0:T(8,128)(2,1)S(1)}, bf16[4,384,768]{2,1,0:T(8,128)(2,1)S(1)}, u32[]{:S(2)}, u32[]{:S(2)}) collective-permute-start(bf16[4,384,768]{2,1,0:T(8,128)(2,1)S(1)} %copy-done.15), channel_id=1, source_target_pairs={{0,16},{16,0},{8,24},{24,8},{1,17},{17,1},{9,25},{25,9},{2,18},{18... | collective-permute-start | bytes 7077896 | tf_op jit(solution)/shard_map/ppermute | solution.py:94
  1155.6 282.8 %all-reduce.10.cloned.1.call-start = ((), (), s32[]{:S(2)}) async-start(), calls=%async_computation.12 | async-start | bytes 196608 | tf_op jit(solution)/shard_map/psum | solution.py:366
  1235.6 66.9 %collective-permute-start.4 = (bf16[1984,768]{1,0:T(8,128)(2,1)}, bf16[1984,768]{1,0:T(8,128)(2,1)}, u32[]{:S(2)}, u32[]{:S(2)}) collective-permute-start(bf16[1984,768]{1,0:T(8,128)(2,1)} %copy.179), channel_id=1, source_target_pairs={{0,4},{4,0},{1,5},{5,1},{2,6},{6,2},{3,7},{7,3},{8,12},{12,8},{9,1... | collective-permute-start | bytes 9142280 | tf_op jit(solution)/shard_map/ppermute | solution.py:44
  1241.2 198.7 %reduce-scatter.9.cloned.1.call-start = ((), (), s32[]{:S(2)}) async-start(), calls=%async_computation.7 | async-start | bytes 3932160 | tf_op jit(solution)/shard_map/reduce_scatter | solution.py:40
  1313.3 258.4 %all-reduce.8.cloned.1.call-start = ((), (), s32[]{:S(2)}) async-start(), calls=%async_computation.11 | async-start | bytes 2359296 | tf_op jit(solution)/shard_map/psum | solution.py:368
  1319.5 39.9 %collective-permute-start.19 = (bf16[4,384,768]{2,1,0:T(8,128)(2,1)}, bf16[4,384,768]{2,1,0:T(8,128)(2,1)}, u32[]{:S(2)}, u32[]{:S(2)}) collective-permute-start(bf16[4,384,768]{2,1,0:T(8,128)(2,1)} %add_convert_fusion.13), channel_id=1, source_target_pairs={{0,8},{8,0},{16,24},{24,16},{1,9},{9,1},{17,25},{25,17},{2,10},{10... | collective-permute-start | bytes 7077896 | tf_op jit(solution)/shard_map/ppermute | solution.py:102
  1319.5 48.9 %collective-permute-start.20 = (bf16[4,384,768]{2,1,0:T(8,128)(2,1)}, bf16[4,384,768]{2,1,0:T(8,128)(2,1)}, u32[]{:S(2)}, u32[]{:S(2)}) collective-permute-start(bf16[4,384,768]{2,1,0:T(8,128)(2,1)} %add_convert_fusion.11), channel_id=1, source_target_pairs={{0,8},{8,0},{16,24},{24,16},{1,9},{9,1},{17,25},{25,17},{2,10},{10... | collective-permute-start | bytes 7077896 | tf_op jit(solution)/shard_map/ppermute | solution.py:102
  1320.1 255.5 %reduce-scatter.15.cloned.1.call-start = ((), (), s32[]{:S(2)}) async-start(), calls=%async_computation.14 | async-start | bytes 3932160
  1320.3 54.8 %collective-permute-start.21 = (bf16[4,384,768]{2,1,0:T(8,128)(2,1)}, bf16[4,384,768]{2,1,0:T(8,128)(2,1)}, u32[]{:S(2)}, u32[]{:S(2)}) collective-permute-start(bf16[4,384,768]{2,1,0:T(8,128)(2,1)} %add_convert_fusion.17), channel_id=1, source_target_pairs={{0,16},{16,0},{8,24},{24,8},{1,17},{17,1},{9,25},{25,9},{2,18},{18... | collective-permute-start | bytes 7077896 | tf_op jit(solution)/shard_map/ppermute | solution.py:94
  1321.9 103.8 %collective-permute-start.27 = (bf16[4,384,768]{2,1,0:T(8,128)(2,1)}, bf16[4,384,768]{2,1,0:T(8,128)(2,1)}, u32[]{:S(2)}, u32[]{:S(2)}) collective-permute-start(bf16[4,384,768]{2,1,0:T(8,128)(2,1)} %add_convert_fusion.16), channel_id=1, source_target_pairs={{0,16},{16,0},{8,24},{24,8},{1,17},{17,1},{9,25},{25,9},{2,18},{18... | collective-permute-start | bytes 7077896 | tf_op jit(solution)/shard_map/ppermute | solution.py:94
  1327.2 53.3 %collective-permute-start.25 = (bf16[4,384,768]{2,1,0:T(8,128)(2,1)}, bf16[4,384,768]{2,1,0:T(8,128)(2,1)}, u32[]{:S(2)}, u32[]{:S(2)}) collective-permute-start(bf16[4,384,768]{2,1,0:T(8,128)(2,1)} %add_convert_fusion.12), channel_id=1, source_target_pairs={{0,8},{8,0},{16,24},{24,16},{1,9},{9,1},{17,25},{25,17},{2,10},{10... | collective-permute-start | bytes 7077896 | tf_op jit(solution)/shard_map/ppermute | solution.py:102
  1359.5 27.8 %collective-permute-start.26 = (bf16[4,384,768]{2,1,0:T(8,128)(2,1)S(1)}, bf16[4,384,768]{2,1,0:T(8,128)(2,1)S(1)}, u32[]{:S(2)}, u32[]{:S(2)}) collective-permute-start(bf16[4,384,768]{2,1,0:T(8,128)(2,1)S(1)} %copy-done.13), channel_id=1, source_target_pairs={{0,8},{8,0},{16,24},{24,16},{1,9},{9,1},{17,25},{25,17},{2,10},{10... | collective-permute-start | bytes 7077896 | tf_op jit(solution)/shard_map/ppermute | solution.py:102
  1368.5 126.8 %collective-permute-start.23 = (bf16[4,384,768]{2,1,0:T(8,128)(2,1)}, bf16[4,384,768]{2,1,0:T(8,128)(2,1)}, u32[]{:S(2)}, u32[]{:S(2)}) collective-permute-start(bf16[4,384,768]{2,1,0:T(8,128)(2,1)} %add_convert_fusion.15), channel_id=1, source_target_pairs={{0,16},{16,0},{8,24},{24,8},{1,17},{17,1},{9,25},{25,9},{2,18},{18... | collective-permute-start | bytes 7077896 | tf_op jit(solution)/shard_map/ppermute | solution.py:94
  1380.4 64.4 %collective-permute-start.22 = (bf16[4,384,768]{2,1,0:T(8,128)(2,1)}, bf16[4,384,768]{2,1,0:T(8,128)(2,1)}, u32[]{:S(2)}, u32[]{:S(2)}) collective-permute-start(bf16[4,384,768]{2,1,0:T(8,128)(2,1)} %get-tuple-element.173), channel_id=1, source_target_pairs={{0,8},{8,0},{16,24},{24,16},{1,9},{9,1},{17,25},{25,17},{2,10},{10... | collective-permute-start | bytes 7077896 | tf_op jit(solution)/shard_map/ppermute | solution.py:102
  1431.1 70.1 %collective-permute-start.28 = (bf16[4,384,768]{2,1,0:T(8,128)(2,1)}, bf16[4,384,768]{2,1,0:T(8,128)(2,1)}, u32[]{:S(2)}, u32[]{:S(2)}) collective-permute-start(bf16[4,384,768]{2,1,0:T(8,128)(2,1)} %get-tuple-element.169), channel_id=1, source_target_pairs={{0,8},{8,0},{16,24},{24,16},{1,9},{9,1},{17,25},{25,17},{2,10},{10... | collective-permute-start | bytes 7077896 | tf_op jit(solution)/shard_map/ppermute | solution.py:102
  1431.1 113.8 %collective-permute-start.29 = (bf16[4,384,768]{2,1,0:T(8,128)(2,1)}, bf16[4,384,768]{2,1,0:T(8,128)(2,1)}, u32[]{:S(2)}, u32[]{:S(2)}) collective-permute-start(bf16[4,384,768]{2,1,0:T(8,128)(2,1)} %add_convert_fusion.14), channel_id=1, source_target_pairs={{0,16},{16,0},{8,24},{24,8},{1,17},{17,1},{9,25},{25,9},{2,18},{18... | collective-permute-start | bytes 7077896 | tf_op jit(solution)/shard_map/ppermute | solution.py:94
  1501.2 96.3 %collective-permute-start.24 = (bf16[4,384,768]{2,1,0:T(8,128)(2,1)}, bf16[4,384,768]{2,1,0:T(8,128)(2,1)}, u32[]{:S(2)}, u32[]{:S(2)}) collective-permute-start(bf16[4,384,768]{2,1,0:T(8,128)(2,1)} %get-tuple-element.171), channel_id=1, source_target_pairs={{0,8},{8,0},{16,24},{24,16},{1,9},{9,1},{17,25},{25,17},{2,10},{10... | collective-permute-start | bytes 7077896 | tf_op jit(solution)/shard_map/ppermute | solution.py:102
  1505.4 45.5 %copy-start.11 = (bf16[1970,768]{1,0:T(8,128)(2,1)S(1)}, bf16[1970,768]{1,0:T(8,128)(2,1)}, u32[]{:S(2)}) copy-start(bf16[1970,768]{1,0:T(8,128)(2,1)} %convolution_convert_fusion) | copy-start | bytes 9077764
  1550.9 50.9 %collective-permute-start.30 = (bf16[4,384,768]{2,1,0:T(8,128)(2,1)}, bf16[4,384,768]{2,1,0:T(8,128)(2,1)}, u32[]{:S(2)}, u32[]{:S(2)}) collective-permute-start(bf16[4,384,768]{2,1,0:T(8,128)(2,1)} %get-tuple-element.167), channel_id=1, source_target_pairs={{0,8},{8,0},{16,24},{24,16},{1,9},{9,1},{17,25},{25,17},{2,10},{10... | collective-permute-start | bytes 7077896 | tf_op jit(solution)/shard_map/ppermute | solution.py:102
  (133 other events, 984.7 us)
Sparse Core Ops, SparseCore 0:
  13.7 63.9 all-gather.7
  137.9 63.5 all-gather.9
  203.6 62.1 all-gather.13
  267.2 29.0 all-gather.11
  818.8 58.6 reduce-scatter.12
  878.9 63.5 all-gather.15
  1155.7 34.9 reduce-scatter.10
  1241.3 120.7 all-reduce.9
  1364.5 61.1 reduce-scatter.8
  1428.0 55.6 all-reduce.7
  1486.1 60.2 reduce-scatter.14
